TPU v7x, 128 devices: a whole 4x4x4 slice. The times are simulated.
128 devices in a mesh: gx: 32 (over y, z, core), gy: 4 (over x).
Axes of the slice: x: 4, y: 4, z: 4, core: 2. Of those that a mesh axis runs over, the one named last changes fastest.
Arguments:
- ice_state: float32 [128, 5, 32, 1024], P(('gx', 'gy')), may hold values from -4 to 4
- thickness: float32 [128, 5, 32, 1024], P(('gx', 'gy')), may hold values from 0.3 to 3
- concentration: float32 [128, 5, 32, 1024], P(('gx', 'gy')), may hold values from 0.04 to 0.2
- cat_mask: int32 [128, 5, 32, 1024], P(('gx', 'gy')), may hold values 0 or 1
- forcing: float32 [16384, 4, 1024], P(('gx', 'gy')), may hold values from -4 to 4
- ice_target: int32 [16384], P(('gx', 'gy')), may hold values from -1 to 4095, as said below
Outputs:
- ice_out: float32 [128, 5, 32, 1024], P(('gx', 'gy'))
- ocean_stress: float32 [16384, 2, 1024], P(('gx', 'gy'))
Inputs may be any that keep to these rules, and one draw needn't show every extreme that they name: `ice_target`: each ice index 0 to 4095 appears exactly once, all others are -1. The ocean blocks of one device carry at most 1 ice blocks of any one cap column, and some device carries exactly 1 of some column.
All inputs are finite; a program needn't handle non-finite values. No bound on the sum of `cat_mask` on one device may be relied on, other than what follows from the above.
Results may differ from a plain program's by a relative error of at most 0.00002.
Values sent between devices are 32-bit elements; how exact they have to be, the bound alone decides.
A program may use at most 128 MiB of HBM per device.

v0:
```python
import jax
import jax.numpy as jnp
from jax import lax
from jax.sharding import PartitionSpec as P

SUB = 8


ELASTIC = 0.5
ECC_SQUARED = 4.0
CREEP = 0.05
PRESSURE_SCALE = 1.0
COMPACTNESS_DECAY = 2.0
BASE_MASS = 0.5
DRAG_COEFF = 1.0
TIME_STEP = 0.5
CORIOLIS = 0.2


def with_halo(block, sides, width):
    for axis, dim in sides:
        count = lax.axis_size(axis)
        forward = [(i, i + 1) for i in range(count - 1)]
        forward.append((count - 1, 0))
        backward = [(target, source) for source, target in forward]
        low = lax.ppermute(
            lax.slice_in_dim(block, block.shape[dim] - width, None, axis=dim), axis, forward
        )
        high = lax.ppermute(lax.slice_in_dim(block, 0, width, axis=dim), axis, backward)
        block = jnp.concatenate([low, block, high], axis=dim)
    return block


def ice_static(thickness, concentration, cat_mask):
    present = cat_mask.astype(jnp.float32)
    ice_fraction = jnp.sum(concentration * present, axis=0)
    ice_volume = jnp.sum(thickness * concentration * present, axis=0)
    ice_mass = ice_volume + BASE_MASS
    ice_strength = PRESSURE_SCALE * ice_volume * jnp.exp(-COMPACTNESS_DECAY * (1.0 - ice_fraction))
    return (ice_fraction, ice_mass, ice_strength)


def stress_update(vel_sides, sig_sum, sig_diff, sig_shear, ice_strength):
    east_side, west_side, north_side, south_side = vel_sides
    stretch_x = 0.5 * (east_side[0] - west_side[0])
    stretch_y = 0.5 * (north_side[1] - south_side[1])
    divergence = stretch_x + stretch_y
    tension = stretch_x - stretch_y
    shearing = 0.5 * (north_side[0] - south_side[0]) + 0.5 * (east_side[1] - west_side[1])
    deform = (
        jnp.sqrt(divergence * divergence + (tension * tension + shearing * shearing) / ECC_SQUARED)
        + CREEP
    )
    damping = ice_strength + ELASTIC * ECC_SQUARED * deform
    new_sum = (ice_strength * sig_sum + ELASTIC * ice_strength * (divergence - deform)) / (
        ice_strength + ELASTIC * deform
    )
    new_diff = (ice_strength * sig_diff + ELASTIC * ice_strength * tension) / damping
    new_shear = (ice_strength * sig_shear + 0.5 * ELASTIC * ice_strength * shearing) / damping
    return (new_sum, new_diff, new_shear)


def momentum_update(vel_east, vel_north, sig_sides, ice_forcing, ice_fraction, ice_mass):
    east_side, west_side, north_side, south_side = sig_sides
    normal_east = 0.5 * (east_side[0] + east_side[1])
    normal_west = 0.5 * (west_side[0] + west_side[1])
    normal_upper = 0.5 * (north_side[0] - north_side[1])
    normal_lower = 0.5 * (south_side[0] - south_side[1])
    force_east = 0.5 * (normal_east - normal_west) + 0.5 * (north_side[2] - south_side[2])
    force_north = 0.5 * (east_side[2] - west_side[2]) + 0.5 * (normal_upper - normal_lower)
    slip_east = ice_forcing[0] - vel_east
    slip_north = ice_forcing[1] - vel_north
    drag_rate = (
        DRAG_COEFF * ice_fraction * jnp.sqrt(slip_east * slip_east + slip_north * slip_north)
    )
    divisor = ice_mass + TIME_STEP * drag_rate
    new_east = (
        ice_mass * vel_east
        + TIME_STEP
        * (
            force_east
            + ice_fraction * ice_forcing[2]
            + drag_rate * ice_forcing[0]
            + CORIOLIS * ice_mass * vel_north
        )
    ) / divisor
    new_north = (
        ice_mass * vel_north
        + TIME_STEP
        * (
            force_north
            + ice_fraction * ice_forcing[3]
            + drag_rate * ice_forcing[1]
            - CORIOLIS * ice_mass * vel_east
        )
    ) / divisor
    return (new_east, new_north)


def ocean_drag(vel_east, vel_north, ice_forcing, ice_fraction):
    slip_east = vel_east - ice_forcing[0]
    slip_north = vel_north - ice_forcing[1]
    drag_rate = (
        DRAG_COEFF * ice_fraction * jnp.sqrt(slip_east * slip_east + slip_north * slip_north)
    )
    return jnp.stack([drag_rate * slip_east, drag_rate * slip_north])


def sides(field, fold_sign, trade_edges, trade_top):
    rim_cells = jnp.stack([field[:, 0], field[:, -1]], axis=1)
    haloed = trade_edges(rim_cells)
    widened = jnp.concatenate([haloed[:, 0:1], field, haloed[:, 3:4]], axis=1)
    east_side = widened[:, 2:]
    west_side = widened[:, :-2]
    partner_top = trade_top(field[:, :, -1])
    folded = fold_sign[:, None] * partner_top[:, ::-1]
    north_side = jnp.concatenate([field[:, :, 1:], folded[:, :, None]], axis=2)
    south_side = jnp.concatenate([jnp.zeros_like(field[:, :, :1]), field[:, :, :-1]], axis=2)
    return (east_side, west_side, north_side, south_side)


def local(ice_state, thickness, concentration, cat_mask, forcing, ice_target):
    devices = lax.axis_size(("gx", "gy"))
    lon_tiles = lax.axis_size("gx")
    state = ice_state[0]
    block_side = state.shape[1]
    latitude_cells = state.shape[2]
    block_rows = latitude_cells // block_side
    cells = block_side * block_side
    slot_capacity = (block_rows + lon_tiles - 1) // lon_tiles
    slot_total = devices * slot_capacity
    listed = forcing.shape[0]
    carried = ice_target >= 0
    owners = jnp.where(carried, ice_target // block_rows, devices)
    ordinal = jnp.arange(listed, dtype=jnp.int32)
    earlier = (owners[:, None] == owners[None, :]) & (ordinal[None, :] < ordinal[:, None])
    rank_in = jnp.sum(earlier.astype(jnp.int32), axis=1)
    send_slot = jnp.where(carried, owners * slot_capacity + rank_in, slot_total)
    source = jnp.full((slot_total,), listed, jnp.int32).at[send_slot].set(ordinal, mode="drop")
    outgoing = jnp.take(forcing, source, axis=0, mode="fill", fill_value=0.0)
    row_tag = (
        jnp.full((slot_total,), -1, jnp.int32)
        .at[send_slot]
        .set(ice_target % block_rows, mode="drop")
    )
    arrived, arrived_rows = (
        lax.all_to_all(outgoing, ("gx", "gy"), split_axis=0, concat_axis=0, tiled=True),
        lax.all_to_all(row_tag, ("gx", "gy"), split_axis=0, concat_axis=0, tiled=True),
    )
    ice_fraction, ice_mass, ice_strength = ice_static(thickness[0], concentration[0], cat_mask[0])
    vel_east, vel_north = (state[0], state[1])
    sig_sum, sig_diff, sig_shear = (state[2], state[3], state[4])
    vel_sign = jnp.array([-1.0, -1.0], dtype=jnp.float32)
    sig_sign = jnp.array([1.0, 1.0, 1.0], dtype=jnp.float32)
    mirror = devices - 1 - lax.axis_index(("gx", "gy"))

    def velocity_edges(rim_cells):
        return with_halo(rim_cells, ((("gx", "gy"), 1),), 1)

    def stress_edges(rim_cells):
        return with_halo(rim_cells, ((("gx", "gy"), 1),), 1)

    def velocity_top(top_row):
        all_tops = lax.all_gather(top_row[None], ("gx", "gy"), axis=0, tiled=True)
        return lax.dynamic_index_in_dim(all_tops, mirror, 0, keepdims=False)

    def stress_top(top_row):
        all_tops = lax.all_gather(top_row[None], ("gx", "gy"), axis=0, tiled=True)
        return lax.dynamic_index_in_dim(all_tops, mirror, 0, keepdims=False)

    slot_of_row = (
        jnp.zeros((block_rows,), jnp.int32)
        .at[jnp.where(arrived_rows >= 0, arrived_rows, block_rows)]
        .set(jnp.arange(slot_total, dtype=jnp.int32), mode="drop")
    )
    row_blocks = arrived[slot_of_row].reshape(block_rows, 4, block_side, block_side)
    ice_forcing = jnp.transpose(row_blocks, (1, 2, 0, 3)).reshape(4, block_side, latitude_cells)
    for subcycle in range(SUB):
        vel_sides = sides(jnp.stack([vel_east, vel_north]), vel_sign, velocity_edges, velocity_top)
        sig_sum, sig_diff, sig_shear = stress_update(
            vel_sides, sig_sum, sig_diff, sig_shear, ice_strength
        )
        sig_sides = sides(
            jnp.stack([sig_sum, sig_diff, sig_shear]), sig_sign, stress_edges, stress_top
        )
        vel_east, vel_north = momentum_update(
            vel_east, vel_north, sig_sides, ice_forcing, ice_fraction, ice_mass
        )
    ice_out = jnp.stack([vel_east, vel_north, sig_sum, sig_diff, sig_shear])[None]
    drag_stress = ocean_drag(vel_east, vel_north, ice_forcing, ice_fraction)
    stress_blocks = jnp.transpose(
        drag_stress.reshape(2, block_side, block_rows, block_side), (2, 0, 1, 3)
    ).reshape(block_rows, 2, cells)
    outbound = jnp.zeros((slot_total, 2, cells), jnp.float32).at[slot_of_row].set(stress_blocks)
    returned = lax.all_to_all(outbound, ("gx", "gy"), split_axis=0, concat_axis=0, tiled=True)
    ocean_stress = jnp.take(returned, send_slot, axis=0, mode="fill", fill_value=0.0)
    return (ice_out, ocean_stress)


def solution(mesh):
    placed = (
        P(("gx", "gy"), None, None, None),
        P(("gx", "gy"), None, None, None),
        P(("gx", "gy"), None, None, None),
        P(("gx", "gy"), None, None, None),
        P(("gx", "gy"), None, None),
        P(("gx", "gy")),
    )
    return jax.shard_map(
        local,
        mesh=mesh,
        in_specs=placed,
        out_specs=(P(("gx", "gy"), None, None, None), P(("gx", "gy"), None, None)),
        check_vma=False,
    )
```

profile of v0, /device:TPU:1, one launch (start us, length us, event | category | flops | bytes accessed | tf_op | source)
XLA Modules:
  0.0 1307.4 jit_solution(3825172993836500524)
XLA Ops:
  4.6 11.5 all-to-all-start.1
  21.4 56.9 %all-gather = f32[256,32,1]{1,2,0:T(1,128)S(1)} all-gather(f32[2,32,1]{1,2,0:T(1,128)S(1)} %copy.273), channel_id=2, replica_groups=mesh['gx'=32,'gy'=4] {'gx','gy'}, dimensions={0}, use_global_device_ids=true | all-gather | bytes 33024 | tf_op jit(solution)/shard_map/all_gather | solution.py:164
  78.4 3.0 gather_fusion
  81.3 3.4 broadcast_select_fusion
  85.0 7.8 all-to-all-start
  100.6 66.3 %all-gather.1 = f32[384,32,1]{1,2,0:T(1,128)S(1)} all-gather(f32[3,32,1]{1,2,0:T(1,128)S(1)} %copy.274), channel_id=3, replica_groups=mesh['gx'=32,'gy'=4] {'gx','gy'}, dimensions={0}, use_global_device_ids=true | all-gather | bytes 49536 | tf_op jit(solution)/shard_map/all_gather | solution.py:168
  173.8 3.2 gather_fusion.1
  196.4 56.9 %all-gather.2 = f32[256,32,1]{1,2,0:T(1,128)S(1)} all-gather(f32[2,32,1]{1,2,0:T(1,128)} %copy.277), channel_id=4, replica_groups=mesh['gx'=32,'gy'=4] {'gx','gy'}, dimensions={0}, use_global_device_ids=true | all-gather | bytes 33024 | tf_op jit(solution)/shard_map/all_gather | solution.py:164
  267.3 67.4 %all-gather.3 = f32[384,32,1]{1,2,0:T(1,128)} all-gather(f32[3,32,1]{1,2,0:T(1,128)S(1)} %copy.278), channel_id=5, replica_groups=mesh['gx'=32,'gy'=4] {'gx','gy'}, dimensions={0}, use_global_device_ids=true | all-gather | bytes 49536 | tf_op jit(solution)/shard_map/all_gather | solution.py:168
  348.7 60.9 %all-gather.4 = f32[256,32,1]{1,2,0:T(1,128)S(1)} all-gather(f32[2,32,1]{1,2,0:T(1,128)} %copy.281), channel_id=6, replica_groups=mesh['gx'=32,'gy'=4] {'gx','gy'}, dimensions={0}, use_global_device_ids=true | all-gather | bytes 33024 | tf_op jit(solution)/shard_map/all_gather | solution.py:164
  419.8 67.1 %all-gather.5 = f32[384,32,1]{1,2,0:T(1,128)} all-gather(f32[3,32,1]{1,2,0:T(1,128)S(1)} %copy.282), channel_id=7, replica_groups=mesh['gx'=32,'gy'=4] {'gx','gy'}, dimensions={0}, use_global_device_ids=true | all-gather | bytes 49536 | tf_op jit(solution)/shard_map/all_gather | solution.py:168
  500.8 60.9 %all-gather.6 = f32[256,32,1]{1,2,0:T(1,128)S(1)} all-gather(f32[2,32,1]{1,2,0:T(1,128)} %copy.285), channel_id=8, replica_groups=mesh['gx'=32,'gy'=4] {'gx','gy'}, dimensions={0}, use_global_device_ids=true | all-gather | bytes 33024 | tf_op jit(solution)/shard_map/all_gather | solution.py:164
  571.1 66.7 %all-gather.7 = f32[384,32,1]{1,2,0:T(1,128)} all-gather(f32[3,32,1]{1,2,0:T(1,128)S(1)} %copy.286), channel_id=9, replica_groups=mesh['gx'=32,'gy'=4] {'gx','gy'}, dimensions={0}, use_global_device_ids=true | all-gather | bytes 49536 | tf_op jit(solution)/shard_map/all_gather | solution.py:168
  651.7 60.9 %all-gather.8 = f32[256,32,1]{1,2,0:T(1,128)S(1)} all-gather(f32[2,32,1]{1,2,0:T(1,128)} %copy.289), channel_id=10, replica_groups=mesh['gx'=32,'gy'=4] {'gx','gy'}, dimensions={0}, use_global_device_ids=true | all-gather | bytes 33024 | tf_op jit(solution)/shard_map/all_gather | solution.py:164
  722.8 66.9 %all-gather.9 = f32[384,32,1]{1,2,0:T(1,128)} all-gather(f32[3,32,1]{1,2,0:T(1,128)S(1)} %copy.290), channel_id=11, replica_groups=mesh['gx'=32,'gy'=4] {'gx','gy'}, dimensions={0}, use_global_device_ids=true | all-gather | bytes 49536 | tf_op jit(solution)/shard_map/all_gather | solution.py:168
  803.4 61.3 %all-gather.10 = f32[256,32,1]{1,2,0:T(1,128)S(1)} all-gather(f32[2,32,1]{1,2,0:T(1,128)} %copy.293), channel_id=12, replica_groups=mesh['gx'=32,'gy'=4] {'gx','gy'}, dimensions={0}, use_global_device_ids=true | all-gather | bytes 33024 | tf_op jit(solution)/shard_map/all_gather | solution.py:164
  874.1 66.7 %all-gather.11 = f32[384,32,1]{1,2,0:T(1,128)} all-gather(f32[3,32,1]{1,2,0:T(1,128)S(1)} %copy.294), channel_id=13, replica_groups=mesh['gx'=32,'gy'=4] {'gx','gy'}, dimensions={0}, use_global_device_ids=true | all-gather | bytes 49536 | tf_op jit(solution)/shard_map/all_gather | solution.py:168
  954.7 60.9 %all-gather.12 = f32[256,32,1]{1,2,0:T(1,128)S(1)} all-gather(f32[2,32,1]{1,2,0:T(1,128)} %copy.297), channel_id=14, replica_groups=mesh['gx'=32,'gy'=4] {'gx','gy'}, dimensions={0}, use_global_device_ids=true | all-gather | bytes 33024 | tf_op jit(solution)/shard_map/all_gather | solution.py:164
  1027.6 66.7 %all-gather.13 = f32[384,32,1]{1,2,0:T(1,128)} all-gather(f32[3,32,1]{1,2,0:T(1,128)S(1)} %copy.298), channel_id=15, replica_groups=mesh['gx'=32,'gy'=4] {'gx','gy'}, dimensions={0}, use_global_device_ids=true | all-gather | bytes 49536 | tf_op jit(solution)/shard_map/all_gather | solution.py:168
  1108.3 59.9 %all-gather.14 = f32[256,32,1]{1,2,0:T(1,128)S(1)} all-gather(f32[2,32,1]{1,2,0:T(1,128)} %copy.301), channel_id=16, replica_groups=mesh['gx'=32,'gy'=4] {'gx','gy'}, dimensions={0}, use_global_device_ids=true | all-gather | bytes 33024 | tf_op jit(solution)/shard_map/all_gather | solution.py:164
  1180.0 66.3 %all-gather.15 = f32[384,32,1]{1,2,0:T(1,128)} all-gather(f32[3,32,1]{1,2,0:T(1,128)S(1)} %copy.302), channel_id=17, replica_groups=mesh['gx'=32,'gy'=4] {'gx','gy'}, dimensions={0}, use_global_device_ids=true | all-gather | bytes 49536 | tf_op jit(solution)/shard_map/all_gather | solution.py:168
  1267.3 3.9 scatter_fusion
  1271.2 12.2 all-to-all-start.2
  1286.1 16.7 %all-to-all-done.2 = f32[128,2,1024]{2,1,0:T(2,128)} async-done(((f32[128,2,1024]{2,1,0:T(2,128)}), f32[128,2,1024]{2,1,0:T(2,128)}, u32[]{:S(2)}, u32[]{:S(2)}) %all-to-all-start.2) | async-done | bytes 1048608 | tf_op jit(solution)/shard_map/all_to_all | solution.py:195
  (503 shorter events, 230.8 us)
Async XLA Ops:
  4.6 80.4 %all-to-all-start.1 = ((s32[128,1,1]{2,1,0:T(1,128)}), s32[128,1,1]{2,1,0:T(1,128)S(1)}, u32[]{:S(2)}, u32[]{:S(2)}) async-start(s32[128,1,1]{2,1,0:T(1,128)} %copy.204), calls=%async_computation.1 | async-start | bytes 131072 | tf_op jit(solution)/shard_map/all_to_all | solution.py:148
  17.1 81.0 %collective-permute-start.1 = (f32[2,1,1024]{2,0,1:T(2,128)S(1)}, f32[2,1,1024]{2,0,1:T(2,128)S(1)}, u32[]{:S(2)}, u32[]{:S(2)}) collective-permute-start(f32[2,1,1024]{2,0,1:T(2,128)S(1)} %copy.272), channel_id=1, source_target_pairs={{0,1},{1,2},{2,3},{3,4},{4,5},{5,6},{6,7},{7,8},{8,9},{9,10},{10,1... | collective-permute-start | bytes 24584 | tf_op jit(solution)/shard_map/ppermute | solution.py:26
  18.6 79.5 %collective-permute-start = (f32[2,1,1024]{2,0,1:T(2,128)S(1)}, f32[2,1,1024]{2,0,1:T(2,128)S(1)}, u32[]{:S(2)}, u32[]{:S(2)}) collective-permute-start(f32[2,1,1024]{2,0,1:T(2,128)S(1)} %copy.271), channel_id=1, source_target_pairs={{1,0},{2,1},{3,2},{4,3},{5,4},{6,5},{7,6},{8,7},{9,8},{10,9},{11,1... | collective-permute-start | bytes 24584 | tf_op jit(solution)/shard_map/ppermute | solution.py:29
  85.0 88.8 %all-to-all-start = ((f32[128,4,1024]{2,1,0:T(4,128)}), f32[128,4,1024]{2,1,0:T(4,128)}, u32[]{:S(2)}, u32[]{:S(2)}) async-start(f32[128,4,1024]{2,1,0:T(4,128)} %broadcast_select_fusion), calls=%async_computation | async-start | bytes 4194304 | tf_op jit(solution)/shard_map/all_to_all | solution.py:147
  169.6 20.3 %collective-permute-start.3 = (f32[3,1,1024]{2,1,0:T(1,128)S(1)}, f32[3,1,1024]{2,1,0:T(1,128)S(1)}, u32[]{:S(2)}, u32[]{:S(2)}) collective-permute-start(f32[3,1,1024]{2,1,0:T(1,128)S(1)} %get-tuple-element.101), channel_id=1, source_target_pairs={{0,1},{1,2},{2,3},{3,4},{4,5},{5,6},{6,7},{7,8},{8,9},{9,10},{10,1... | collective-permute-start | bytes 36872 | tf_op jit(solution)/shard_map/ppermute | solution.py:26
  170.5 19.4 %collective-permute-start.2 = (f32[3,1,1024]{2,1,0:T(1,128)S(1)}, f32[3,1,1024]{2,1,0:T(1,128)S(1)}, u32[]{:S(2)}, u32[]{:S(2)}) collective-permute-start(f32[3,1,1024]{2,1,0:T(1,128)S(1)} %get-tuple-element.100), channel_id=1, source_target_pairs={{1,0},{2,1},{3,2},{4,3},{5,4},{6,5},{7,6},{8,7},{9,8},{10,9},{11,1... | collective-permute-start | bytes 36872 | tf_op jit(solution)/shard_map/ppermute | solution.py:29
  257.0 5.8 collective-permute-start.5
  339.2 4.5 collective-permute-start.6
  491.4 4.5 collective-permute-start.10
  563.0 4.6 collective-permute-start.13
  563.1 4.5 collective-permute-start.12
  794.2 4.5 collective-permute-start.18
  866.1 4.6 collective-permute-start.21
  866.2 4.5 collective-permute-start.20
  945.2 4.5 collective-permute-start.22
  1017.0 4.6 collective-permute-start.25
  1017.0 4.5 collective-permute-start.24
  1098.7 5.7 collective-permute-start.27
  1098.7 5.7 collective-permute-start.26
  1169.5 5.5 collective-permute-start.29
  1169.6 5.5 collective-permute-start.28
  1250.8 5.7 collective-permute-start.31
  1250.8 5.7 collective-permute-start.30
  1271.2 31.6 %all-to-all-start.2 = ((f32[128,2,1024]{2,1,0:T(2,128)}), f32[128,2,1024]{2,1,0:T(2,128)}, u32[]{:S(2)}, u32[]{:S(2)}) async-start(f32[128,2,1024]{2,1,0:T(2,128)} %scatter_fusion), calls=%async_computation.2 | async-start | bytes 2097152 | tf_op jit(solution)/shard_map/all_to_all | solution.py:195
  (102 other events, 2278.7 us)
where the time goes:
time: 1320 us; the launch traced here: 1310 us
  blocking collectives  1010 us (77%)
  local copies, waits for them, and re-layouts  104 us (8%)
  other arithmetic  91.4 us (7%)
  starting transfers between devices  79.5 us (6%)
  waiting for transfers between devices  17.6 us (1%)
    all_gather x8, blocking collectives, stress_top(): all_tops = lax.all_gather(top_row[None], ('gx', 'gy'), axis=0, tiled=True)  534 us
    all_gather x8, blocking collectives, velocity_top(): all_tops = lax.all_gather(top_row[None], ('gx', 'gy'), axis=0, tiled=True)  478 us
    ppermute x16, starting transfers between devices, with_halo(): lax.ppermute(lax.slice_in_dim(block, 0, width, axis=dim), axis, backward)  43.9 us
  transfers between devices with their start and end apart: 35, of which 3 were waited for; matrix products, arithmetic and copies ran while one was open for 5% of the time, Pallas kernels for 0%

commit v1 on v0

v1 whole, which is shorter than its diff:
```python
import jax
import jax.numpy as jnp
from jax import lax
from jax.experimental import pallas as pl
from jax.experimental.pallas import tpu as pltpu
from jax.sharding import PartitionSpec as P

MESH = pl.DeviceIdType.MESH
SUB = 8
HALF = 4
H = 2 * HALF
NLON = 32
W = NLON + 2 * H
OWN = H * 8
END = OWN + NLON * 8
NDEV = 128
RB = 33
PER = W // 8
F32 = jnp.float32


def at(d):
    return (d // 4, d % 4)


def rot(x, shift, axis):
    return pltpu.roll(x, shift % x.shape[axis], axis)


def iota(shape, axis):
    return lax.broadcasted_iota(jnp.int32, shape, axis)


def within(i, count):
    return jnp.minimum(jnp.maximum(i, 0), count - 1)


def root(x):
    return x * lax.rsqrt(jnp.maximum(x, 1e-30))


def stress(due_x, dun_y, due_y, dun_x, ss, sd, sh, strength):
    plus = due_x + dun_y
    minus = due_x - dun_y
    cross = due_y + dun_x
    deform = 0.5 * root(plus * plus + 0.25 * (minus * minus + cross * cross)) + 0.05
    ss = strength * (ss + 0.25 * plus - 0.5 * deform) / (strength + 0.5 * deform)
    scaled = strength / (strength + 2.0 * deform)
    sd = scaled * (sd + 0.25 * minus)
    sh = scaled * (sh + 0.125 * cross)
    return ss, sd, sh


def momentum(ue, un, dxx_x, dsh_y, dsh_x, dyy_y, uo, vo, wx, wy, cover, mass):
    force_east = 0.25 * dxx_x + 0.5 * dsh_y
    force_north = 0.5 * dsh_x + 0.25 * dyy_y
    a = uo - ue
    b = vo - un
    drag = cover * root(a * a + b * b)
    inv = 1.0 / (mass + 0.5 * drag)
    tenth = 0.1 * mass
    east = mass * ue + 0.5 * (force_east + cover * wx + drag * uo) + tenth * un
    north = mass * un + 0.5 * (force_north + cover * wy + drag * vo) - tenth * ue
    return east * inv, north * inv


def quads(x0, x1, x2, x3, group):
    low = (group % 2) == 0
    y0 = jnp.where(low, x0, rot(x1, 32, 1))
    y1 = jnp.where(low, rot(x0, -32, 1), x1)
    y2 = jnp.where(low, x2, rot(x3, 32, 1))
    y3 = jnp.where(low, rot(x2, -32, 1), x3)
    low = group < 2
    return (
        jnp.where(low, y0, rot(y2, 64, 1)),
        jnp.where(low, y1, rot(y3, 64, 1)),
        jnp.where(low, rot(y0, -64, 1), y2),
        jnp.where(low, rot(y1, -64, 1), y3),
    )


def kernel(
    tgt, state, thick, conc, mask, forc, ice_out, ocean_out,
    tgt_s, tgt_v, idx_v, idx_s, dst_v, dst_s,
    r_state, r_thick, r_conc, r_mask, fv, outb, arr, tagm,
    st, sc, fo, sp, spc, spf,
    t7, e7, t4, e4, t5, e5, h5,
    dr, sb, out2, ret, ice_v,
    in_sem, loc_sem, a_sem, r_sem, x_send, x_recv,
):
    gx, gy = lax.axis_index("gx"), lax.axis_index("gy")
    me = gx * 4 + gy
    y, z, core, x = gx // 8, (gx // 2) % 4, gx % 2, gy
    sx, sz, sy = 1 - 2 * (x % 2), 1 - 2 * (z % 2), 1 - 2 * (y % 2)

    def peer(k):
        k = (k * 37) % 128
        px = (x + sx * (k % 4) + 4) % 4
        pc = (core + (k // 4) % 2) % 2
        pz = (z + sz * ((k // 8) % 4) + 4) % 4
        py = (y + sy * (k // 32) + 4) % 4
        return (py * 4 + pz) * 2 + pc, px

    loads = [
        pltpu.make_async_copy(src, dst, in_sem.at[i])
        for i, (src, dst) in enumerate(
            [(tgt, tgt_v), (tgt, tgt_s), (thick, r_thick), (conc, r_conc), (mask, r_mask), (state, r_state), (forc, fv)]
        )
    ]
    for load in loads:
        load.start()

    barrier = pltpu.get_barrier_semaphore()

    def greet(k, carry):
        d = (me + k) % NDEV
        pl.semaphore_signal(barrier, inc=1, device_id=at(d), device_id_type=MESH)
        return carry

    lax.fori_loop(1, NDEV, greet, 0)

    square = (NDEV, NDEV)
    lane_sq, sub_sq = iota(square, 1), iota(square, 0)
    loads[0].wait()
    loads[1].wait()
    row = jnp.broadcast_to(tgt_v[...].astype(F32), square)
    column = jnp.sum(jnp.where(lane_sq == sub_sq, row, 0.0), axis=1, keepdims=True)
    target = jnp.broadcast_to(column, square).astype(jnp.int32)
    hit = (target >= 0) & (target // 32 == lane_sq)
    listed = jnp.sum(jnp.where(hit, sub_sq.astype(F32), 0.0), axis=0, keepdims=True)
    place = jnp.sum(jnp.where(hit, (target % 32 + 1).astype(F32), 0.0), axis=0, keepdims=True) - 1.0
    idx_v[0:1, :] = listed.astype(jnp.int32)
    idx_v[1:2, :] = place.astype(jnp.int32)
    to_smem = pltpu.make_async_copy(idx_v, idx_s, loc_sem.at[0])
    to_smem.start()

    for load in loads[2:6]:
        load.wait()

    def relay(n, carry):
        lb, chunk = n // 8, n % 8
        rows, lanes = pl.ds(pl.multiple_of(lb * 8, 8), 8), pl.ds(pl.multiple_of(chunk * 128, 128), 128)
        dst = pl.ds(OWN + lb * 64 + chunk, 8, stride=8)
        cover = jnp.zeros((8, 128), F32)
        volume = jnp.zeros((8, 128), F32)
        for cat in range(5):
            part = r_conc[cat, rows, lanes] * r_mask[cat, rows, lanes].astype(F32)
            cover = cover + part
            volume = volume + r_thick[cat, rows, lanes] * part
        sc[0, dst, :] = cover
        sc[1, dst, :] = volume
        for ch in range(5):
            st[ch, dst, :] = r_state[ch, rows, lanes]
        return carry

    lax.fori_loop(0, 32, relay, 0)

    lane8, sub8 = iota((8, 128), 1), iota((8, 128), 0)

    def turned(v):
        for bit in (1, 2, 4):
            v = jnp.where((sub8 // bit) % 2 == 1, rot(v, bit, 0), rot(v, -bit, 0))
        for bit in (1, 2, 4):
            v = jnp.where((lane8 // bit) % 2 == 1, rot(v, bit, 1), rot(v, -bit, 1))
        return v

    def tops(dst, first, src, signs):
        def group(g, carry):
            start = OWN + (24 - 8 * g) * 8 + 7
            for ch, sign in enumerate(signs):
                v = turned(src[ch, pl.ds(start, 8, stride=8), :])
                dst[first + ch, pl.ds(pl.multiple_of(g * 8, 8), 8), :] = v if sign > 0 else -v
            return carry

        lax.fori_loop(0, 4, group, 0)

    def strip(dst, src, ext, first, count):
        for ch in range(count):
            for b in range(PER):
                own = rot(src[ch, pl.ds(b * 8 + 7, 8, stride=8 * PER), :], -H, 1)
                far = ext[first + ch, pl.ds(b, 8, stride=PER), :]
                dst[ch, b * 8 : b * 8 + 8, :] = jnp.where(lane8 < 128 - H, own, far)

    def merge():
        for ch in range(5):
            for b in range(PER):
                where = pl.ds(b * 8 + 7, 8, stride=8 * PER)
                new = rot(sp[ch, b * 8 : b * 8 + 8, :], H, 1)
                st[ch, where, :] = jnp.where(lane8 >= 128 - H, new, st[ch, where, :])

    tops(t7, 0, st, (-1, -1, 1, 1, 1))
    tops(t7, 5, sc, (1, 1))

    west, east = (me + NDEV - 1) % NDEV, (me + 1) % NDEV
    over, over_east, over_west = NDEV - 1 - me, (NDEV - me) % NDEV, (2 * NDEV - 2 - me) % NDEV

    def remote(src, dst, d, i):
        return pltpu.make_async_remote_copy(
            src_ref=src, dst_ref=dst, send_sem=x_send.at[i], recv_sem=x_recv.at[i],
            device_id=at(d), device_id_type=MESH,
        )

    def beside(ref, to_west, to_east, i):
        return [
            (remote(ref.at[:, pl.ds(OWN, OWN)], to_west, west, i), None, None),
            (remote(ref.at[:, pl.ds(END - OWN, OWN)], to_east, east, i + 1), None, None),
        ]

    def across(t, e, i):
        parts = []
        for n, (d, src, dst) in enumerate(
            [
                (over, t, e.at[:, pl.ds(H, NLON)]),
                (over_east, t.at[:, pl.ds(NLON - H, H)], e.at[:, pl.ds(0, H)]),
                (over_west, t.at[:, pl.ds(0, H)], e.at[:, pl.ds(NLON + H, H)]),
            ]
        ):
            here = pltpu.make_async_copy(src, dst, x_recv.at[i + n]) if n else None
            parts.append((remote(src, dst, d, i + n), here, d))
        return parts

    def start(copies):
        for copy, here, d in copies:
            if here is None:
                copy.start()
            else:
                pl.when(d != me)(copy.start)
                pl.when(d == me)(here.start)

    def landed(copies):
        for copy, _, _ in copies:
            copy.wait_recv()

    def left(copies):
        for copy, here, d in copies:
            if here is None:
                copy.wait_send()
            else:
                pl.when(d != me)(copy.wait_send)

    first = (
        beside(st, st.at[:, pl.ds(END, OWN)], st.at[:, pl.ds(0, OWN)], 0)
        + beside(
            sc.at[pl.ds(0, 2)],
            sc.at[pl.ds(0, 2), pl.ds(END, OWN)],
            sc.at[pl.ds(0, 2), pl.ds(0, OWN)],
            2,
        )
        + across(t7, e7, 4)
    )
    second = beside(fo, fo.at[:, pl.ds(END, OWN)], fo.at[:, pl.ds(0, OWN)], 7) + across(t4, e4, 9)
    third = beside(st, h5.at[1], h5.at[0], 12) + across(t5, e5, 14)

    to_smem.wait()
    loads[6].wait()

    def pack(c, carry):
        outb[c, 0:32, :] = fv[within(idx_s[0, c], NDEV)]
        outb[c, 32:33, :] = jnp.full((1, 128), idx_s[1, c].astype(F32))
        return carry

    lax.fori_loop(0, NDEV, pack, 0, unroll=4)

    pl.semaphore_wait(barrier, NDEV - 1)
    start(first)

    def send(k, carry):
        a, b = peer(k)
        pltpu.make_async_remote_copy(
            src_ref=outb.at[a * 4 + b], dst_ref=arr.at[me], send_sem=a_sem.at[0], recv_sem=a_sem.at[1],
            device_id=(a, b), device_id_type=MESH,
        ).start()
        return carry

    lax.fori_loop(1, NDEV, send, 0)
    own_block = pltpu.make_async_copy(outb.at[me], arr.at[me], loc_sem.at[1])
    own_block.start()

    shape2 = (2, 8, 128)
    lane2, sub2 = iota(shape2, 2), iota(shape2, 1)

    def get(ref, ch, r):
        return ref[ch, pl.ds(pl.multiple_of(r, 8), 16), :].reshape(shape2)

    def put(ref, ch, r, v):
        ref[ch, pl.ds(pl.multiple_of(r, 8), 16), :] = v.reshape(16, 128)

    def diff_lon(ref, ch, r):
        return get(ref, ch, r + 8) - get(ref, ch, r - 8)

    def diff_lat(v):
        up = rot(v, -1, 2)
        up = jnp.where(lane2 == 127, rot(up, -1, 1), up)
        down = rot(v, 1, 2)
        down = jnp.where(lane2 == 0, jnp.where(sub2 == 0, 0.0, rot(down, 1, 1)), down)
        return up - down

    def strip_lon(v):
        upper = jnp.concatenate([v[1:], rot(v[:1], -1, 1)], axis=0)
        lower = jnp.concatenate([rot(v[-1:], 1, 1), v[:-1]], axis=0)
        return upper - lower

    def strip_lat(v):
        return rot(v, -1, 2) - rot(v, 1, 2)

    def whole(ref, ch):
        return ref[ch].reshape(PER, 8, 128)

    def keep(ref, ch, v):
        ref[ch] = v.reshape(PER * 8, 128)

    def sweep(lo, hi, body):
        def step(n, carry):
            body((lo + 2 * n) * 8)
            return carry

        lax.fori_loop(0, (hi - lo) // 2, step, 0)

    def strength_of(volume, cover):
        return volume * jnp.exp(-2.0 * (1.0 - cover))

    def stress_step(m):
        def body(r):
            ue, un = get(st, 0, r), get(st, 1, r)
            new = stress(
                diff_lon(st, 0, r), diff_lat(un), diff_lat(ue), diff_lon(st, 1, r),
                get(st, 2, r), get(st, 3, r), get(st, 4, r), get(sc, 2, r),
            )
            for ch in range(3):
                put(st, 2 + ch, r, new[ch])

        sweep(1 + 2 * m, W - 1 - 2 * m, body)
        ue, un = whole(sp, 0), whole(sp, 1)
        new = stress(
            strip_lon(ue), strip_lat(un), strip_lat(ue), strip_lon(un),
            whole(sp, 2), whole(sp, 3), whole(sp, 4), whole(spc, 2),
        )
        for ch in range(3):
            keep(sp, 2 + ch, new[ch])

    def momentum_step(m):
        def body(r):
            ss, sd, sh = get(st, 2, r), get(st, 3, r), get(st, 4, r)
            dxx = diff_lon(st, 2, r) + diff_lon(st, 3, r)
            new = momentum(
                get(st, 0, r), get(st, 1, r), dxx, diff_lat(sh), diff_lon(st, 4, r), diff_lat(ss - sd),
                get(fo, 0, r), get(fo, 1, r), get(fo, 2, r), get(fo, 3, r), get(sc, 0, r), get(sc, 1, r),
            )
            put(st, 0, r, new[0])
            put(st, 1, r, new[1])

        sweep(2 + 2 * m, W - 2 - 2 * m, body)
        ss, sd, sh = whole(sp, 2), whole(sp, 3), whole(sp, 4)
        new = momentum(
            whole(sp, 0), whole(sp, 1), strip_lon(ss + sd), strip_lat(sh), strip_lon(sh), strip_lat(ss - sd),
            whole(spf, 0), whole(spf, 1), whole(spf, 2), whole(spf, 3), whole(spc, 0), whole(spc, 1),
        )
        keep(sp, 0, new[0])
        keep(sp, 1, new[1])

    landed(first)
    left(first)
    strip(sp, st, e7, 0, 5)
    strip(spc, sc, e7, 5, 2)

    def statics(r):
        cover, volume = get(sc, 0, r), get(sc, 1, r)
        put(sc, 1, r, volume + 0.5)
        put(sc, 2, r, strength_of(volume, cover))

    sweep(0, W, statics)
    cover, volume = whole(spc, 0), whole(spc, 1)
    keep(spc, 1, volume + 0.5)
    keep(spc, 2, strength_of(volume, cover))
    stress_step(0)

    own_block.wait()
    some = pltpu.make_async_remote_copy(
        src_ref=outb.at[pl.ds(0, NDEV - 1)], dst_ref=arr.at[pl.ds(0, NDEV - 1)],
        send_sem=a_sem.at[0], recv_sem=a_sem.at[1], device_id=(gx, gy), device_id_type=MESH,
    )
    some.wait_recv()

    def tag(s, carry):
        tagm[pl.ds(s, 1), :] = arr[s, 32:33, :]
        return carry

    lax.fori_loop(0, NDEV, tag, 0, unroll=8)
    tags = tagm[...]
    origin = jnp.sum(jnp.where(tags.astype(jnp.int32) == lane_sq, sub_sq.astype(F32), 0.0), axis=0, keepdims=True)
    back = jnp.sum(jnp.where(sub_sq == lane_sq, tags, 0.0), axis=0, keepdims=True)
    dst_v[0:1, :] = origin.astype(jnp.int32)
    dst_v[1:2, :] = jnp.maximum(back, 0.0).astype(jnp.int32)
    to_smem = pltpu.make_async_copy(dst_v, dst_s, loc_sem.at[2])
    to_smem.start()
    to_smem.wait()

    group8 = lane8 // 32

    def place_rows(chunk, carry):
        sources = [within(dst_s[0, chunk * 4 + j], NDEV) for j in range(4)]
        for ch in range(4):
            rows = quads(*[arr[s, pl.ds(ch, 8, stride=4), :] for s in sources], group8)
            for p in range(4):
                fo[ch, pl.ds(OWN + p * 8 + chunk, 8, stride=32), :] = rows[p]
        return carry

    lax.fori_loop(0, 8, place_rows, 0)
    tops(t4, 0, fo, (-1, -1, -1, -1))
    start(second)
    landed(second)
    strip(spf, fo, e4, 0, 4)

    momentum_step(0)
    for m in range(1, HALF):
        stress_step(m)
        momentum_step(m)

    merge()
    tops(t5, 0, st, (-1, -1, 1, 1, 1))
    start(third)
    landed(third)
    left(third)
    for ch in range(5):
        st[ch, 0:OWN, :] = h5[0, ch]
        st[ch, END:, :] = h5[1, ch]
    strip(sp, st, e5, 0, 5)
    for m in range(HALF):
        stress_step(m)
        momentum_step(m)
    merge()

    def drag(r):
        a = get(st, 0, r) - get(fo, 0, r)
        b = get(st, 1, r) - get(fo, 1, r)
        rate = get(sc, 0, r) * root(a * a + b * b)
        put(dr, 0, r - OWN, rate * a)
        put(dr, 1, r - OWN, rate * b)

    sweep(H, H + NLON, drag)

    def blocks(chunk, carry):
        for ch in range(2):
            rows = quads(*[dr[ch, pl.ds(p * 8 + chunk, 8, stride=32), :] for p in range(4)], group8)
            for j in range(4):
                sb[chunk * 4 + j, pl.ds(ch, 8, stride=2), :] = rows[j]
        return carry

    lax.fori_loop(0, 8, blocks, 0)

    def give(k, carry):
        a, b = peer(k)
        d = a * 4 + b
        out2[d] = sb[within(dst_s[1, d], 32)]
        pltpu.make_async_remote_copy(
            src_ref=out2.at[d], dst_ref=ret.at[me], send_sem=r_sem.at[0], recv_sem=r_sem.at[1],
            device_id=(a, b), device_id_type=MESH,
        ).start()
        return carry

    lax.fori_loop(1, NDEV, give, 0)
    ret[me] = sb[within(dst_s[1, me], 32)]

    def lay_out(n, carry):
        lb, chunk = n // 8, n % 8
        rows, lanes = pl.ds(pl.multiple_of(lb * 8, 8), 8), pl.ds(pl.multiple_of(chunk * 128, 128), 128)
        for ch in range(5):
            ice_v[ch, rows, lanes] = st[ch, pl.ds(OWN + lb * 64 + chunk, 8, stride=8), :]
        return carry

    lax.fori_loop(0, 32, lay_out, 0)
    store = pltpu.make_async_copy(ice_v, ice_out, loc_sem.at[3])
    store.start()

    left(second)
    some.wait_send()
    some = pltpu.make_async_remote_copy(
        src_ref=out2.at[pl.ds(0, NDEV - 1)], dst_ref=ret.at[pl.ds(0, NDEV - 1)],
        send_sem=r_sem.at[0], recv_sem=r_sem.at[1], device_id=(gx, gy), device_id_type=MESH,
    )
    some.wait_recv()

    def unpack(b, carry):
        t = tgt_s[0, b]
        v = ret[within(t // 32, NDEV)]
        ocean_out[b] = jnp.where(t >= 0, v, 0.0)
        return carry

    lax.fori_loop(0, NDEV, unpack, 0, unroll=4)
    store.wait()
    some.wait_send()


def local(ice_state, thickness, concentration, cat_mask, forcing, ice_target):
    blocks = forcing.reshape(NDEV, 4, 8, 128).transpose(0, 2, 1, 3).reshape(NDEV, 32, 128)
    hbm = pl.BlockSpec(memory_space=pl.ANY)
    vmem, dma = pltpu.VMEM, pltpu.SemaphoreType.DMA

    def v(*shape, dtype=F32):
        return vmem(shape, dtype)

    raw = (5, NLON, 1024)
    rows = W * 8
    ice, ocean = pl.pallas_call(
        kernel,
        out_shape=(
            jax.ShapeDtypeStruct(raw, F32),
            jax.ShapeDtypeStruct((NDEV, 16, 128), F32),
        ),
        in_specs=[hbm] * 6,
        out_specs=(hbm, pl.BlockSpec(memory_space=vmem)),
        scratch_shapes=[
            pltpu.SMEM((1, 128), jnp.int32), v(1, 128, dtype=jnp.int32),
            v(8, 128, dtype=jnp.int32), pltpu.SMEM((8, 128), jnp.int32),
            v(8, 128, dtype=jnp.int32), pltpu.SMEM((8, 128), jnp.int32),
            v(*raw), v(*raw), v(*raw), v(*raw, dtype=jnp.int32),
            v(NDEV, 32, 128), v(NDEV, RB, 128), v(NDEV, RB, 128), v(NDEV, 128),
            v(5, rows, 128), v(3, rows, 128), v(4, rows, 128),
            v(5, W, 128), v(3, W, 128), v(4, W, 128),
            v(7, NLON, 128), v(7, W, 128), v(4, NLON, 128), v(4, W, 128), v(5, NLON, 128), v(5, W, 128),
            v(2, 5, OWN, 128),
            v(2, NLON * 8, 128), v(32, 16, 128), v(NDEV, 16, 128), v(NDEV, 16, 128), v(*raw),
            dma((7,)), dma((4,)), dma((2,)), dma((2,)), dma((17,)), dma((17,)),
        ],
        compiler_params=pltpu.CompilerParams(
            collective_id=0, has_side_effects=True, vmem_limit_bytes=48 * 2**20
        ),
        name="ice",
    )(ice_target.reshape(1, NDEV), ice_state[0], thickness[0], concentration[0], cat_mask[0], blocks)
    ocean = ocean.reshape(NDEV, 8, 2, 128).transpose(0, 2, 1, 3).reshape(NDEV, 2, 1024)
    return ice[None], ocean


def solution(mesh):
    lead = ("gx", "gy")
    four, three = P(lead, None, None, None), P(lead, None, None)
    return jax.shard_map(
        local,
        mesh=mesh,
        in_specs=(four, four, four, four, three, P(lead)),
        out_specs=(four, three),
        check_vma=False,
    )
```

time: 1320 us -> 125 us (0.09)
  blocking collectives: 1010 us -> 0 us
  Pallas kernels: 0 us -> 117 us
  local copies, waits for them, and re-layouts: 104 us -> 6.8 us
  other arithmetic: 91.4 us -> 0 us
  starting transfers between devices: 79.5 us -> 0 us
  waiting for transfers between devices: 17.6 us -> 0 us
    all_gather x16 -> x0, blocking collectives: 1010 us -> none  [the longest x8 534 us: stress_top(): all_tops = lax.all_gather(top_row[None], ('gx', 'gy'), axis=0, tiled=True)]
    pallas_call x0 -> x1, Pallas kernels: none -> 117 us  [local(): pl.pallas_call(kernel, out_shape=(jax.ShapeDtypeStruct(raw, F32), jax.Sha...]
    ppermute x32 -> x0, starting transfers between devices: 48 us -> none  [the longest x16 43.9 us: with_halo(): lax.ppermute(lax.slice_in_dim(block, 0, width, axis=dim), axis, backward)]
    div x30 -> x0, other arithmetic: 36.4 us -> none  [the longest x8 11 us: stress_update(): (ice_strength * sig_sum + ELASTIC * ice_strength * (divergence - deform))...]
    all_to_all x3 -> x0, starting transfers between devices: 31.6 us -> none  [the longest x1 12.2 us: local(): lax.all_to_all(outbound, ('gx', 'gy'), split_axis=0, concat_axis=0, tiled...]
    all_gather x8 -> x0, other arithmetic: 20.5 us -> none  [stress_top(): all_tops = lax.all_gather(top_row[None], ('gx', 'gy'), axis=0, tiled=True)]
    all_to_all x3 -> x0, waiting for transfers between devices: 16.7 us -> none  [the longest x1 16.7 us: local(): lax.all_to_all(outbound, ('gx', 'gy'), split_axis=0, concat_axis=0, tiled...]
    squeeze x21 -> x0, local copies, waits for them, and re-layouts: 16.7 us -> none  [the longest x8 5.96 us: stress_top(): return lax.dynamic_index_in_dim(all_tops, mirror, 0, keepdims=False)]
  transfers between devices with their start and end apart: 35 -> 0, of which waited for: 3 -> 0; matrix products, arithmetic and copies ran while one was open for 5% -> 0% of each run, Pallas kernels for 0% -> 0%
where the time goes in v1:
time: 125 us; the launch traced here: 124 us
  Pallas kernels  117 us (94%)
  local copies, waits for them, and re-layouts  6.8 us (5%)
    pallas_call x1, Pallas kernels, local(): pl.pallas_call(kernel, out_shape=(jax.ShapeDtypeStruct(raw, F32), jax.Sha...  117 us
    unnamed x12, local copies, waits for them, and re-layouts  6.8 us

profile of v1, /device:TPU:1, one launch (start us, length us, event | category | flops | bytes accessed | tf_op | source)
XLA Modules:
  0.0 124.2 jit_solution(18429037231529845361)
XLA Ops:
  0.6 0.0 copy-start
  0.6 1.1 copy-done
  1.7 0.0 copy-start.1
  1.7 1.1 copy-done.1
  2.8 0.0 copy-start.2
  2.8 1.1 copy-done.2
  3.9 0.0 copy-start.3
  3.9 1.1 copy-done.3
  5.0 0.0 copy-start.4
  5.0 0.7 copy-done.4
  5.6 116.8 %ice.1 = (f32[5,32,1024]{2,1,0:T(8,128)S(1)}, f32[128,16,128]{2,1,0:T(8,128)S(1)}) custom-call(s32[1,128]{1,0:T(1,128)S(1)} %bitcast.22, f32[5,32,1024]{2,1,0:T(8,128)S(1)} %bitcast.17, f32[5,32,1024]{2,1,0:T(8,128)S(1)} %bitcast.18, f32[5,32,1024]{2,1,0:T(8,128)S(1)} %bitcast.19, s32[5,32,1024]{2,1,0:T(8,128)S(1)} %bitcast.20, f32[128,32,128]{2,1,0:T(8,128)} %bitcast.23), custom_call_target="tpu_custom_call" | custom-call | tf_op jit(solution)/shard_map/ice/pallas_call | solution.py:504
  122.4 0.8 copy.12
  123.2 1.0 copy.13
Async XLA Ops:
  0.6 1.1 copy-start
  1.7 1.1 copy-start.1
  2.8 1.1 copy-start.2
  3.9 1.1 copy-start.3
  5.0 0.7 copy-start.4

commit v2 on v1

--- a/solution.py
+++ b/solution.py
@@ -84,22 +84,41 @@
     tgt_s, tgt_v, idx_v, idx_s, dst_v, dst_s,
     r_state, r_thick, r_conc, r_mask, fv, outb, arr, tagm,
     st, sc, fo, sp, spc, spf,
-    t7, e7, t4, e4, t5, e5, h5,
+    t7, p7, t4, p4, t5, p5, ext, edge, h5,
     dr, sb, out2, ret, ice_v,
     in_sem, loc_sem, a_sem, r_sem, x_send, x_recv,
 ):
     gx, gy = lax.axis_index("gx"), lax.axis_index("gy")
     me = gx * 4 + gy
     y, z, core, x = gx // 8, (gx // 2) % 4, gx % 2, gy
-    sx, sz, sy = 1 - 2 * (x % 2), 1 - 2 * (z % 2), 1 - 2 * (y % 2)
-
-    def peer(k):
-        k = (k * 37) % 128
-        px = (x + sx * (k % 4) + 4) % 4
-        pc = (core + (k // 4) % 2) % 2
-        pz = (z + sz * ((k // 8) % 4) + 4) % 4
-        py = (y + sy * (k // 32) + 4) % 4
-        return (py * 4 + pz) * 2 + pc, px
+
+    def flipped(bit, by):
+        return 1 - bit if by else bit
+
+    low = []
+    for n in range(16):
+        n = (n * 5) % 16
+        px = 2 * flipped(x // 2, (n // 2) % 2) + flipped(x % 2, n % 2)
+        low.append((2 * flipped(z % 2, (n // 8) % 2) + flipped(core, (n // 4) % 2), px))
+
+    def for_peers(act):
+        def turn(q, carry):
+            high = []
+            for r in range(8):
+                m = (q + r) % 8
+                z1 = (z // 2 + m) % 2
+                y0 = (y + m // 2) % 2
+                y1 = (y // 2 + m // 4) % 2
+                high.append(8 * (2 * y1 + y0) + 4 * z1)
+            for n in range(16):
+                a, b = high[(3 * n) % 8] + low[n][0], low[n][1]
+                if n:
+                    act(a, b)
+                else:
+                    pl.when(q != 0)(lambda a=a, b=b: act(a, b))
+            return carry
+
+        lax.fori_loop(0, 8, turn, 0)
 
     loads = [
         pltpu.make_async_copy(src, dst, in_sem.at[i])
@@ -112,12 +131,19 @@
 
     barrier = pltpu.get_barrier_semaphore()
 
-    def greet(k, carry):
-        d = (me + k) % NDEV
-        pl.semaphore_signal(barrier, inc=1, device_id=at(d), device_id_type=MESH)
-        return carry
-
-    lax.fori_loop(1, NDEV, greet, 0)
+    def greet(a, b):
+        pl.semaphore_signal(barrier, inc=1, device_id=(a, b), device_id_type=MESH)
+
+    for b in range(1, 4):
+        greet(gx, (gy + b) % 4)
+
+    def greet_all(k, carry):
+        a = (gx + k) % 32
+        for b in range(4):
+            greet(a, b)
+        return carry
+
+    lax.fori_loop(1, 32, greet_all, 0)
 
     square = (NDEV, NDEV)
     lane_sq, sub_sq = iota(square, 1), iota(square, 0)
@@ -164,22 +190,42 @@
             v = jnp.where((lane8 // bit) % 2 == 1, rot(v, bit, 1), rot(v, -bit, 1))
         return v
 
-    def tops(dst, first, src, signs):
-        def group(g, carry):
-            start = OWN + (24 - 8 * g) * 8 + 7
-            for ch, sign in enumerate(signs):
-                v = turned(src[ch, pl.ds(start, 8, stride=8), :])
-                dst[first + ch, pl.ds(pl.multiple_of(g * 8, 8), 8), :] = v if sign > 0 else -v
-            return carry
-
-        lax.fori_loop(0, 4, group, 0)
-
-    def strip(dst, src, ext, first, count):
+    def tops(dst, parts):
+        full = []
+        for n, (src, ch, sign) in enumerate([part for part in parts for _ in range(4)]):
+            g, q = n % 4, n % 16
+            v = rot(src[ch, pl.ds(OWN + (24 - 8 * g) * 8 + 7, 8, stride=8), :], 8 * q + 8, 1)
+            v = v if sign > 0 else -v
+            if q == 0:
+                full.append(v)
+            else:
+                full[-1] = jnp.where(lane8 // 8 == q, v, full[-1])
+        for n, v in enumerate(full):
+            dst[8 * n : 8 * n + 8, :] = turned(v)
+
+    def beyond(packed, count):
+        for ch in range(count):
+            for k in range(6):
+                source, g = (1, 3) if k == 0 else (2, 0) if k == 5 else (0, k - 1)
+                n = ch * 4 + g
+                v = packed[source, 8 * (n // 16) : 8 * (n // 16) + 8, :]
+                ext[ch, 8 * k : 8 * k + 8, :] = rot(v, 120 - 8 * (n % 16), 1)
+
+    def strip_own(dst, src, count, fresh=None):
         for ch in range(count):
             for b in range(PER):
-                own = rot(src[ch, pl.ds(b * 8 + 7, 8, stride=8 * PER), :], -H, 1)
+                v = rot(src[ch, pl.ds(b * 8 + 7, 8, stride=8 * PER), :], -H, 1)
+                if fresh is not None:
+                    lon = sub8 * PER + b
+                    v = jnp.where((lon < H) | (lon >= H + NLON), v, dst[ch, b * 8 : b * 8 + 8, :])
+                dst[ch, b * 8 : b * 8 + 8, :] = v
+
+    def strip_far(dst, first, count):
+        for ch in range(count):
+            for b in range(PER):
+                where = slice(b * 8, b * 8 + 8)
                 far = ext[first + ch, pl.ds(b, 8, stride=PER), :]
-                dst[ch, b * 8 : b * 8 + 8, :] = jnp.where(lane8 < 128 - H, own, far)
+                dst[ch, where, :] = jnp.where(lane8 < 128 - H, dst[ch, where, :], far)
 
     def merge():
         for ch in range(5):
@@ -188,8 +234,8 @@
                 new = rot(sp[ch, b * 8 : b * 8 + 8, :], H, 1)
                 st[ch, where, :] = jnp.where(lane8 >= 128 - H, new, st[ch, where, :])
 
-    tops(t7, 0, st, (-1, -1, 1, 1, 1))
-    tops(t7, 5, sc, (1, 1))
+    state_parts = [(st, 0, -1), (st, 1, -1), (st, 2, 1), (st, 3, 1), (st, 4, 1)]
+    tops(t7, state_parts + [(sc, 0, 1), (sc, 1, 1)])
 
     west, east = (me + NDEV - 1) % NDEV, (me + 1) % NDEV
     over, over_east, over_west = NDEV - 1 - me, (NDEV - me) % NDEV, (2 * NDEV - 2 - me) % NDEV
@@ -200,23 +246,23 @@
             device_id=at(d), device_id_type=MESH,
         )
 
-    def beside(ref, to_west, to_east, i):
+    def beside(to_west, to_east, at_west, at_east, i):
         return [
-            (remote(ref.at[:, pl.ds(OWN, OWN)], to_west, west, i), None, None),
-            (remote(ref.at[:, pl.ds(END - OWN, OWN)], to_east, east, i + 1), None, None),
+            (remote(to_west, at_east, west, i), None, None),
+            (remote(to_east, at_west, east, i + 1), None, None),
         ]
 
-    def across(t, e, i):
+    def halo(ref, count, i):
+        def part(lon):
+            return ref.at[pl.ds(0, count), pl.ds(lon * 8, OWN)]
+
+        return beside(part(H), part(NLON), part(0), part(H + NLON), i)
+
+    def across(t, p, i):
         parts = []
-        for n, (d, src, dst) in enumerate(
-            [
-                (over, t, e.at[:, pl.ds(H, NLON)]),
-                (over_east, t.at[:, pl.ds(NLON - H, H)], e.at[:, pl.ds(0, H)]),
-                (over_west, t.at[:, pl.ds(0, H)], e.at[:, pl.ds(NLON + H, H)]),
-            ]
-        ):
-            here = pltpu.make_async_copy(src, dst, x_recv.at[i + n]) if n else None
-            parts.append((remote(src, dst, d, i + n), here, d))
+        for n, d in enumerate([over, over_east, over_west]):
+            here = pltpu.make_async_copy(t, p.at[n], x_recv.at[i + n]) if n else None
+            parts.append((remote(t, p.at[n], d, i + n), here, d))
         return parts
 
     def start(copies):
@@ -238,18 +284,9 @@
             else:
                 pl.when(d != me)(copy.wait_send)
 
-    first = (
-        beside(st, st.at[:, pl.ds(END, OWN)], st.at[:, pl.ds(0, OWN)], 0)
-        + beside(
-            sc.at[pl.ds(0, 2)],
-            sc.at[pl.ds(0, 2), pl.ds(END, OWN)],
-            sc.at[pl.ds(0, 2), pl.ds(0, OWN)],
-            2,
-        )
-        + across(t7, e7, 4)
-    )
-    second = beside(fo, fo.at[:, pl.ds(END, OWN)], fo.at[:, pl.ds(0, OWN)], 7) + across(t4, e4, 9)
-    third = beside(st, h5.at[1], h5.at[0], 12) + across(t5, e5, 14)
+    first = halo(st, 5, 0) + halo(sc, 2, 2) + across(t7, p7, 4)
+    second = halo(fo, 4, 7) + across(t4, p4, 9)
+    third = beside(edge.at[0], edge.at[1], h5.at[0], h5.at[1], 12) + across(t5, p5, 14)
 
     to_smem.wait()
     loads[6].wait()
@@ -264,36 +301,32 @@
     pl.semaphore_wait(barrier, NDEV - 1)
     start(first)
 
-    def send(k, carry):
-        a, b = peer(k)
+    def send(a, b):
         pltpu.make_async_remote_copy(
             src_ref=outb.at[a * 4 + b], dst_ref=arr.at[me], send_sem=a_sem.at[0], recv_sem=a_sem.at[1],
             device_id=(a, b), device_id_type=MESH,
         ).start()
-        return carry
-
-    lax.fori_loop(1, NDEV, send, 0)
+
+    for_peers(send)
     own_block = pltpu.make_async_copy(outb.at[me], arr.at[me], loc_sem.at[1])
     own_block.start()
 
-    shape2 = (2, 8, 128)
-    lane2, sub2 = iota(shape2, 2), iota(shape2, 1)
-
-    def get(ref, ch, r):
-        return ref[ch, pl.ds(pl.multiple_of(r, 8), 16), :].reshape(shape2)
-
-    def put(ref, ch, r, v):
-        ref[ch, pl.ds(pl.multiple_of(r, 8), 16), :] = v.reshape(16, 128)
-
-    def diff_lon(ref, ch, r):
-        return get(ref, ch, r + 8) - get(ref, ch, r - 8)
-
-    def diff_lat(v):
-        up = rot(v, -1, 2)
-        up = jnp.where(lane2 == 127, rot(up, -1, 1), up)
-        down = rot(v, 1, 2)
-        down = jnp.where(lane2 == 0, jnp.where(sub2 == 0, 0.0, rot(down, 1, 1)), down)
-        return up - down
+    def get(ref, ch, r, n, shift=0):
+        return ref[ch, pl.ds(pl.multiple_of(r, 8) + shift, 8 * n), :]
+
+    def put(ref, ch, r, n, v):
+        ref[ch, pl.ds(pl.multiple_of(r, 8), 8 * n), :] = v
+
+    def diff_lon(ref, ch, r, n):
+        return get(ref, ch, r + 8, n) - get(ref, ch, r - 8, n)
+
+    def diff_lat(ref, ch, r, n):
+        v = get(ref, ch, r, n)
+        lane, sub = iota(v.shape, 1), iota(v.shape, 0) % 8
+        up = jnp.where(lane == 0, get(ref, ch, r, n, 1), v)
+        down = jnp.where(sub == 0, 0.0, get(ref, ch, r, n, -1))
+        down = jnp.where(lane == 127, down, v)
+        return rot(up, -1, 1) - rot(down, 1, 1)
 
     def strip_lon(v):
         upper = jnp.concatenate([v[1:], rot(v[:1], -1, 1)], axis=0)
@@ -310,26 +343,29 @@
         ref[ch] = v.reshape(PER * 8, 128)
 
     def sweep(lo, hi, body):
-        def step(n, carry):
-            body((lo + 2 * n) * 8)
+        def step(i, carry):
+            body((lo + 4 * i) * 8, 4)
             return carry
 
-        lax.fori_loop(0, (hi - lo) // 2, step, 0)
+        count = (hi - lo) // 4
+        if count:
+            lax.fori_loop(0, count, step, 0)
+        if (hi - lo) % 4:
+            body((lo + 4 * count) * 8, (hi - lo) % 4)
 
     def strength_of(volume, cover):
         return volume * jnp.exp(-2.0 * (1.0 - cover))
 
-    def stress_step(m):
-        def body(r):
-            ue, un = get(st, 0, r), get(st, 1, r)
-            new = stress(
-                diff_lon(st, 0, r), diff_lat(un), diff_lat(ue), diff_lon(st, 1, r),
-                get(st, 2, r), get(st, 3, r), get(st, 4, r), get(sc, 2, r),
-            )
-            for ch in range(3):
-                put(st, 2 + ch, r, new[ch])
-
-        sweep(1 + 2 * m, W - 1 - 2 * m, body)
+    def stress_at(r, n):
+        new = stress(
+            diff_lon(st, 0, r, n), diff_lat(st, 1, r, n), diff_lat(st, 0, r, n), diff_lon(st, 1, r, n),
+            get(st, 2, r, n), get(st, 3, r, n), get(st, 4, r, n), get(sc, 2, r, n),
+        )
+        for ch in range(3):
+            put(st, 2 + ch, r, n, new[ch])
+        put(st, 5, r, n, new[0] - new[1])
+
+    def stress_strip():
         ue, un = whole(sp, 0), whole(sp, 1)
         new = stress(
             strip_lon(ue), strip_lat(un), strip_lat(ue), strip_lon(un),
@@ -338,18 +374,17 @@
         for ch in range(3):
             keep(sp, 2 + ch, new[ch])
 
-    def momentum_step(m):
-        def body(r):
-            ss, sd, sh = get(st, 2, r), get(st, 3, r), get(st, 4, r)
-            dxx = diff_lon(st, 2, r) + diff_lon(st, 3, r)
-            new = momentum(
-                get(st, 0, r), get(st, 1, r), dxx, diff_lat(sh), diff_lon(st, 4, r), diff_lat(ss - sd),
-                get(fo, 0, r), get(fo, 1, r), get(fo, 2, r), get(fo, 3, r), get(sc, 0, r), get(sc, 1, r),
-            )
-            put(st, 0, r, new[0])
-            put(st, 1, r, new[1])
-
-        sweep(2 + 2 * m, W - 2 - 2 * m, body)
+    def momentum_at(r, n):
+        dxx = diff_lon(st, 2, r, n) + diff_lon(st, 3, r, n)
+        new = momentum(
+            get(st, 0, r, n), get(st, 1, r, n),
+            dxx, diff_lat(st, 4, r, n), diff_lon(st, 4, r, n), diff_lat(st, 5, r, n),
+            get(fo, 0, r, n), get(fo, 1, r, n), get(fo, 2, r, n), get(fo, 3, r, n), get(sc, 0, r, n), get(sc, 1, r, n),
+        )
+        put(st, 0, r, n, new[0])
+        put(st, 1, r, n, new[1])
+
+    def momentum_strip():
         ss, sd, sh = whole(sp, 2), whole(sp, 3), whole(sp, 4)
         new = momentum(
             whole(sp, 0), whole(sp, 1), strip_lon(ss + sd), strip_lat(sh), strip_lon(sh), strip_lat(ss - sd),
@@ -360,19 +395,23 @@
 
     landed(first)
     left(first)
-    strip(sp, st, e7, 0, 5)
-    strip(spc, sc, e7, 5, 2)
-
-    def statics(r):
-        cover, volume = get(sc, 0, r), get(sc, 1, r)
-        put(sc, 1, r, volume + 0.5)
-        put(sc, 2, r, strength_of(volume, cover))
+    beyond(p7, 7)
+    strip_own(sp, st, 5)
+    strip_far(sp, 0, 5)
+    strip_own(spc, sc, 2)
+    strip_far(spc, 5, 2)
+
+    def statics(r, n):
+        cover, volume = get(sc, 0, r, n), get(sc, 1, r, n)
+        put(sc, 1, r, n, volume + 0.5)
+        put(sc, 2, r, n, strength_of(volume, cover))
 
     sweep(0, W, statics)
     cover, volume = whole(spc, 0), whole(spc, 1)
     keep(spc, 1, volume + 0.5)
     keep(spc, 2, strength_of(volume, cover))
-    stress_step(0)
+    sweep(1, W - 1, stress_at)
+    stress_strip()
 
     own_block.wait()
     some = pltpu.make_async_remote_copy(
@@ -406,36 +445,71 @@
         return carry
 
     lax.fori_loop(0, 8, place_rows, 0)
-    tops(t4, 0, fo, (-1, -1, -1, -1))
+    tops(t4, [(fo, 0, -1), (fo, 1, -1), (fo, 2, -1), (fo, 3, -1)])
     start(second)
+
+    sweep(H, H + NLON, momentum_at)
+    for m in range(1, HALF):
+        sweep(H - 1 + 2 * m, W - H + 1 - 2 * m, stress_at)
+        sweep(H + 2 * m, W - H - 2 * m, momentum_at)
+
     landed(second)
-    strip(spf, fo, e4, 0, 4)
-
-    momentum_step(0)
-    for m in range(1, HALF):
-        stress_step(m)
-        momentum_step(m)
+    beyond(p4, 4)
+    strip_own(spf, fo, 4)
+    strip_far(spf, 0, 4)
+
+    def rims(first_lon, width, body):
+        for lon in (first_lon, W - first_lon - width):
+            for n in range(0, width, 4):
+                body((lon + n) * 8, min(4, width - n))
+
+    rims(2, H - 2, momentum_at)
+    momentum_strip()
+
+    def rest_one(m, carry):
+        rims(1 + 2 * m, H - 2, stress_at)
+        stress_strip()
+        rims(2 + 2 * m, H - 2, momentum_at)
+        momentum_strip()
+        return carry
+
+    lax.fori_loop(1, HALF, rest_one, 0)
 
     merge()
-    tops(t5, 0, st, (-1, -1, 1, 1, 1))
+    tops(t5, state_parts)
+    for ch in range(5):
+        edge[0, ch] = st[ch, OWN : 2 * OWN, :]
+        edge[1, ch] = st[ch, END - OWN : END, :]
     start(third)
+    strip_own(sp, st, 5)
+    for m in range(HALF):
+        sweep(H + 1 + 2 * m, W - H - 1 - 2 * m, stress_at)
+        sweep(H + 2 + 2 * m, W - H - 2 - 2 * m, momentum_at)
+
     landed(third)
-    left(third)
     for ch in range(5):
         st[ch, 0:OWN, :] = h5[0, ch]
         st[ch, END:, :] = h5[1, ch]
-    strip(sp, st, e5, 0, 5)
-    for m in range(HALF):
-        stress_step(m)
-        momentum_step(m)
+    beyond(p5, 5)
+    strip_own(sp, st, 5, True)
+    strip_far(sp, 0, 5)
+
+    def rest_two(m, carry):
+        rims(1 + 2 * m, H, stress_at)
+        stress_strip()
+        rims(2 + 2 * m, H, momentum_at)
+        momentum_strip()
+        return carry
+
+    lax.fori_loop(0, HALF, rest_two, 0)
     merge()
 
-    def drag(r):
-        a = get(st, 0, r) - get(fo, 0, r)
-        b = get(st, 1, r) - get(fo, 1, r)
-        rate = get(sc, 0, r) * root(a * a + b * b)
-        put(dr, 0, r - OWN, rate * a)
-        put(dr, 1, r - OWN, rate * b)
+    def drag(r, n):
+        a = get(st, 0, r, n) - get(fo, 0, r, n)
+        b = get(st, 1, r, n) - get(fo, 1, r, n)
+        rate = get(sc, 0, r, n) * root(a * a + b * b)
+        put(dr, 0, r - OWN, n, rate * a)
+        put(dr, 1, r - OWN, n, rate * b)
 
     sweep(H, H + NLON, drag)
 
@@ -448,17 +522,15 @@
 
     lax.fori_loop(0, 8, blocks, 0)
 
-    def give(k, carry):
-        a, b = peer(k)
+    def give(a, b):
         d = a * 4 + b
         out2[d] = sb[within(dst_s[1, d], 32)]
         pltpu.make_async_remote_copy(
             src_ref=out2.at[d], dst_ref=ret.at[me], send_sem=r_sem.at[0], recv_sem=r_sem.at[1],
             device_id=(a, b), device_id_type=MESH,
         ).start()
-        return carry
-
-    lax.fori_loop(1, NDEV, give, 0)
+
+    for_peers(give)
     ret[me] = sb[within(dst_s[1, me], 32)]
 
     def lay_out(n, carry):
@@ -473,6 +545,7 @@
     store.start()
 
     left(second)
+    left(third)
     some.wait_send()
     some = pltpu.make_async_remote_copy(
         src_ref=out2.at[pl.ds(0, NDEV - 1)], dst_ref=ret.at[pl.ds(0, NDEV - 1)],
@@ -493,7 +566,7 @@
 
 def local(ice_state, thickness, concentration, cat_mask, forcing, ice_target):
     blocks = forcing.reshape(NDEV, 4, 8, 128).transpose(0, 2, 1, 3).reshape(NDEV, 32, 128)
-    hbm = pl.BlockSpec(memory_space=pl.ANY)
+    hbm = pl.BlockSpec(memory_space=pltpu.HBM)
     vmem, dma = pltpu.VMEM, pltpu.SemaphoreType.DMA
 
     def v(*shape, dtype=F32):
@@ -508,22 +581,22 @@
             jax.ShapeDtypeStruct((NDEV, 16, 128), F32),
         ),
         in_specs=[hbm] * 6,
-        out_specs=(hbm, pl.BlockSpec(memory_space=vmem)),
+        out_specs=(pl.BlockSpec(memory_space=pl.ANY), pl.BlockSpec(memory_space=vmem)),
         scratch_shapes=[
             pltpu.SMEM((1, 128), jnp.int32), v(1, 128, dtype=jnp.int32),
             v(8, 128, dtype=jnp.int32), pltpu.SMEM((8, 128), jnp.int32),
             v(8, 128, dtype=jnp.int32), pltpu.SMEM((8, 128), jnp.int32),
             v(*raw), v(*raw), v(*raw), v(*raw, dtype=jnp.int32),
             v(NDEV, 32, 128), v(NDEV, RB, 128), v(NDEV, RB, 128), v(NDEV, 128),
-            v(5, rows, 128), v(3, rows, 128), v(4, rows, 128),
+            v(6, rows, 128), v(3, rows, 128), v(4, rows, 128),
             v(5, W, 128), v(3, W, 128), v(4, W, 128),
-            v(7, NLON, 128), v(7, W, 128), v(4, NLON, 128), v(4, W, 128), v(5, NLON, 128), v(5, W, 128),
-            v(2, 5, OWN, 128),
+            v(16, 128), v(3, 16, 128), v(8, 128), v(3, 8, 128), v(16, 128), v(3, 16, 128), v(7, W, 128),
+            v(2, 5, OWN, 128), v(2, 5, OWN, 128),
             v(2, NLON * 8, 128), v(32, 16, 128), v(NDEV, 16, 128), v(NDEV, 16, 128), v(*raw),
             dma((7,)), dma((4,)), dma((2,)), dma((2,)), dma((17,)), dma((17,)),
         ],
         compiler_params=pltpu.CompilerParams(
-            collective_id=0, has_side_effects=True, vmem_limit_bytes=48 * 2**20
+            collective_id=0, has_side_effects=True, vmem_limit_bytes=58 * 2**20
         ),
         name="ice",
     )(ice_target.reshape(1, NDEV), ice_state[0], thickness[0], concentration[0], cat_mask[0], blocks)

time: 125 us -> 89.6 us (0.72)
  Pallas kernels: 117 us -> 84.5 us
  local copies, waits for them, and re-layouts: 6.8 us -> 4.25 us
    pallas_call x1, Pallas kernels: 117 us -> 84.5 us  [local(): pl.pallas_call(kernel, out_shape=(jax.ShapeDtypeStruct(raw, F32), jax.Sha...]
    unnamed x12 -> x2, local copies, waits for them, and re-layouts: 6.8 us -> 4.25 us
where the time goes in v2:
time: 89.6 us; the launch traced here: 89.4 us
  Pallas kernels  84.5 us (94%)
  local copies, waits for them, and re-layouts  4.25 us (5%)
    pallas_call x1, Pallas kernels, local(): pl.pallas_call(kernel, out_shape=(jax.ShapeDtypeStruct(raw, F32), jax.Sha...  84.5 us
    unnamed x2, local copies, waits for them, and re-layouts  4.25 us

profile of v2, /device:TPU:1, one launch (start us, length us, event | category | flops | bytes accessed | tf_op | source)
XLA Modules:
  0.0 89.4 jit_solution(9457202948084368757)
XLA Ops:
  0.6 84.5 %ice.1 = (f32[5,32,1024]{2,1,0:T(8,128)}, f32[128,16,128]{2,1,0:T(8,128)}) custom-call(s32[1,128]{1,0:T(1,128)} %bitcast.23, f32[5,32,1024]{2,1,0:T(8,128)} %bitcast.18, f32[5,32,1024]{2,1,0:T(8,128)} %bitcast.19, f32[5,32,1024]{2,1,0:T(8,128)} %bitcast.20, s32[5,32,1024]{2,1,0:T(8,128)} %bitcast.21, f32[128,32,128]{2,1,0:T(8,128)} %bitcast.16), custom_call_target="tpu_custom_call" | custom-call | tf_op jit(solution)/shard_map/ice/pallas_call | solution.py:577
  85.2 2.0 %copy.12 = f32[1,5,32,1024]{3,2,1,0:T(8,128)} copy(f32[1,5,32,1024]{3,2,1,0:T(8,128)} %bitcast.22) | data formatting | bytes 1310720
  87.2 2.3 %copy.13 = f32[128,2,1024]{2,1,0:T(2,128)} copy(f32[128,2,1024]{2,1,0:T(2,128)} %bitcast.17) | data formatting | bytes 2097152

commit v3 on v2

--- a/solution.py
+++ b/solution.py
@@ -80,12 +80,12 @@
 
 
 def kernel(
-    tgt, state, thick, conc, mask, forc, ice_out, ocean_out,
-    tgt_s, tgt_v, idx_v, idx_s, dst_v, dst_s,
+    tgt, state, thick, conc, mask, forc, ice_out, ret,
+    tgt_v, idx_v, idx_s, dst_v, dst_s,
     r_state, r_thick, r_conc, r_mask, fv, outb, arr, tagm,
     st, sc, fo, sp, spc, spf,
-    t7, p7, t4, p4, t5, p5, ext, edge, h5,
-    dr, sb, out2, ret, ice_v,
+    t7, p7, t4, p4, t5, p5, ext, edge, h5, edge7, h7,
+    dr, sb, out2, ice_v,
     in_sem, loc_sem, a_sem, r_sem, x_send, x_recv,
 ):
     gx, gy = lax.axis_index("gx"), lax.axis_index("gy")
@@ -97,7 +97,7 @@
 
     low = []
     for n in range(16):
-        n = (n * 5) % 16
+        n = (n * 11) % 16
         px = 2 * flipped(x // 2, (n // 2) % 2) + flipped(x % 2, n % 2)
         low.append((2 * flipped(z % 2, (n // 8) % 2) + flipped(core, (n // 4) % 2), px))
 
@@ -123,7 +123,7 @@
     loads = [
         pltpu.make_async_copy(src, dst, in_sem.at[i])
         for i, (src, dst) in enumerate(
-            [(tgt, tgt_v), (tgt, tgt_s), (thick, r_thick), (conc, r_conc), (mask, r_mask), (state, r_state), (forc, fv)]
+            [(tgt, tgt_v), (thick, r_thick), (conc, r_conc), (mask, r_mask), (state, r_state), (forc, fv)]
         )
     ]
     for load in loads:
@@ -148,7 +148,6 @@
     square = (NDEV, NDEV)
     lane_sq, sub_sq = iota(square, 1), iota(square, 0)
     loads[0].wait()
-    loads[1].wait()
     row = jnp.broadcast_to(tgt_v[...].astype(F32), square)
     column = jnp.sum(jnp.where(lane_sq == sub_sq, row, 0.0), axis=1, keepdims=True)
     target = jnp.broadcast_to(column, square).astype(jnp.int32)
@@ -160,7 +159,7 @@
     to_smem = pltpu.make_async_copy(idx_v, idx_s, loc_sem.at[0])
     to_smem.start()
 
-    for load in loads[2:6]:
+    for load in loads[1:5]:
         load.wait()
 
     def relay(n, carry):
@@ -236,6 +235,10 @@
 
     state_parts = [(st, 0, -1), (st, 1, -1), (st, 2, 1), (st, 3, 1), (st, 4, 1)]
     tops(t7, state_parts + [(sc, 0, 1), (sc, 1, 1)])
+    for ch in range(7):
+        src, n = (st, ch) if ch < 5 else (sc, ch - 5)
+        edge7[0, ch] = src[n, OWN : 2 * OWN, :]
+        edge7[1, ch] = src[n, END - OWN : END, :]
 
     west, east = (me + NDEV - 1) % NDEV, (me + 1) % NDEV
     over, over_east, over_west = NDEV - 1 - me, (NDEV - me) % NDEV, (2 * NDEV - 2 - me) % NDEV
@@ -284,12 +287,12 @@
             else:
                 pl.when(d != me)(copy.wait_send)
 
-    first = halo(st, 5, 0) + halo(sc, 2, 2) + across(t7, p7, 4)
+    first = beside(edge7.at[0], edge7.at[1], h7.at[0], h7.at[1], 0) + across(t7, p7, 4)
     second = halo(fo, 4, 7) + across(t4, p4, 9)
     third = beside(edge.at[0], edge.at[1], h5.at[0], h5.at[1], 12) + across(t5, p5, 14)
 
     to_smem.wait()
-    loads[6].wait()
+    loads[5].wait()
 
     def pack(c, carry):
         outb[c, 0:32, :] = fv[within(idx_s[0, c], NDEV)]
@@ -299,7 +302,6 @@
     lax.fori_loop(0, NDEV, pack, 0, unroll=4)
 
     pl.semaphore_wait(barrier, NDEV - 1)
-    start(first)
 
     def send(a, b):
         pltpu.make_async_remote_copy(
@@ -308,6 +310,7 @@
         ).start()
 
     for_peers(send)
+    start(first)
     own_block = pltpu.make_async_copy(outb.at[me], arr.at[me], loc_sem.at[1])
     own_block.start()
 
@@ -393,25 +396,33 @@
         keep(sp, 0, new[0])
         keep(sp, 1, new[1])
 
-    landed(first)
-    left(first)
-    beyond(p7, 7)
-    strip_own(sp, st, 5)
-    strip_far(sp, 0, 5)
-    strip_own(spc, sc, 2)
-    strip_far(spc, 5, 2)
-
     def statics(r, n):
         cover, volume = get(sc, 0, r, n), get(sc, 1, r, n)
         put(sc, 1, r, n, volume + 0.5)
         put(sc, 2, r, n, strength_of(volume, cover))
 
-    sweep(0, W, statics)
-    cover, volume = whole(spc, 0), whole(spc, 1)
-    keep(spc, 1, volume + 0.5)
-    keep(spc, 2, strength_of(volume, cover))
-    sweep(1, W - 1, stress_at)
-    stress_strip()
+    def rims(first_lon, width, body):
+        for lon in (first_lon, W - first_lon - width):
+            for n in range(0, width, 4):
+                body((lon + n) * 8, min(4, width - n))
+
+    def inner(done):
+        for m in range(HALF):
+            if m or not done:
+                sweep(H + 1 + 2 * m, W - H - 1 - 2 * m, stress_at)
+            sweep(H + 2 + 2 * m, W - H - 2 - 2 * m, momentum_at)
+
+    def outer(m, carry):
+        rims(1 + 2 * m, H, stress_at)
+        stress_strip()
+        rims(2 + 2 * m, H, momentum_at)
+        momentum_strip()
+        return carry
+
+    strip_own(sp, st, 5)
+    strip_own(spc, sc, 2)
+    sweep(H, H + NLON, statics)
+    sweep(H + 1, W - H - 1, stress_at)
 
     own_block.wait()
     some = pltpu.make_async_remote_copy(
@@ -444,37 +455,32 @@
                 fo[ch, pl.ds(OWN + p * 8 + chunk, 8, stride=32), :] = rows[p]
         return carry
 
-    lax.fori_loop(0, 8, place_rows, 0)
+    lax.fori_loop(0, 8, place_rows, 0, unroll=2)
     tops(t4, [(fo, 0, -1), (fo, 1, -1), (fo, 2, -1), (fo, 3, -1)])
     start(second)
 
-    sweep(H, H + NLON, momentum_at)
-    for m in range(1, HALF):
-        sweep(H - 1 + 2 * m, W - H + 1 - 2 * m, stress_at)
-        sweep(H + 2 * m, W - H - 2 * m, momentum_at)
-
+    inner(1)
+
+    landed(first)
+    for ch in range(7):
+        dst, n = (st, ch) if ch < 5 else (sc, ch - 5)
+        dst[n, 0:OWN, :] = h7[0, ch]
+        dst[n, END:, :] = h7[1, ch]
+    beyond(p7, 7)
+    strip_own(sp, st, 5, True)
+    strip_far(sp, 0, 5)
+    strip_own(spc, sc, 2, True)
+    strip_far(spc, 5, 2)
+    rims(0, H, statics)
+    cover, volume = whole(spc, 0), whole(spc, 1)
+    keep(spc, 1, volume + 0.5)
+    keep(spc, 2, strength_of(volume, cover))
     landed(second)
     beyond(p4, 4)
     strip_own(spf, fo, 4)
     strip_far(spf, 0, 4)
 
-    def rims(first_lon, width, body):
-        for lon in (first_lon, W - first_lon - width):
-            for n in range(0, width, 4):
-                body((lon + n) * 8, min(4, width - n))
-
-    rims(2, H - 2, momentum_at)
-    momentum_strip()
-
-    def rest_one(m, carry):
-        rims(1 + 2 * m, H - 2, stress_at)
-        stress_strip()
-        rims(2 + 2 * m, H - 2, momentum_at)
-        momentum_strip()
-        return carry
-
-    lax.fori_loop(1, HALF, rest_one, 0)
-
+    lax.fori_loop(0, HALF, outer, 0)
     merge()
     tops(t5, state_parts)
     for ch in range(5):
@@ -482,9 +488,7 @@
         edge[1, ch] = st[ch, END - OWN : END, :]
     start(third)
     strip_own(sp, st, 5)
-    for m in range(HALF):
-        sweep(H + 1 + 2 * m, W - H - 1 - 2 * m, stress_at)
-        sweep(H + 2 + 2 * m, W - H - 2 - 2 * m, momentum_at)
+    inner(0)
 
     landed(third)
     for ch in range(5):
@@ -494,14 +498,7 @@
     strip_own(sp, st, 5, True)
     strip_far(sp, 0, 5)
 
-    def rest_two(m, carry):
-        rims(1 + 2 * m, H, stress_at)
-        stress_strip()
-        rims(2 + 2 * m, H, momentum_at)
-        momentum_strip()
-        return carry
-
-    lax.fori_loop(0, HALF, rest_two, 0)
+    lax.fori_loop(0, HALF, outer, 0)
     merge()
 
     def drag(r, n):
@@ -520,7 +517,7 @@
                 sb[chunk * 4 + j, pl.ds(ch, 8, stride=2), :] = rows[j]
         return carry
 
-    lax.fori_loop(0, 8, blocks, 0)
+    lax.fori_loop(0, 8, blocks, 0, unroll=4)
 
     def give(a, b):
         d = a * 4 + b
@@ -531,7 +528,9 @@
         ).start()
 
     for_peers(give)
-    ret[me] = sb[within(dst_s[1, me], 32)]
+    out2[me] = sb[within(dst_s[1, me], 32)]
+    own_stress = pltpu.make_async_copy(out2.at[me], ret.at[me], loc_sem.at[1])
+    own_stress.start()
 
     def lay_out(n, carry):
         lb, chunk = n // 8, n % 8
@@ -544,6 +543,7 @@
     store = pltpu.make_async_copy(ice_v, ice_out, loc_sem.at[3])
     store.start()
 
+    left(first)
     left(second)
     left(third)
     some.wait_send()
@@ -553,20 +553,44 @@
     )
     some.wait_recv()
 
+    own_stress.wait()
+    store.wait()
+    some.wait_send()
+
+
+def hand_out(tgt, ice, ret, ice_out, ocean_out, tgt_s, ret_v, ice_v, ocean_v, sem):
+    loads = [
+        pltpu.make_async_copy(src, dst, sem.at[i])
+        for i, (src, dst) in enumerate([(tgt, tgt_s), (ret, ret_v), (ice, ice_v)])
+    ]
+    for load in loads:
+        load.start()
+    store = pltpu.make_async_copy(ice_v, ice_out, sem.at[3])
+    loads[2].wait()
+    store.start()
+    loads[0].wait()
+    loads[1].wait()
+
     def unpack(b, carry):
         t = tgt_s[0, b]
-        v = ret[within(t // 32, NDEV)]
-        ocean_out[b] = jnp.where(t >= 0, v, 0.0)
-        return carry
-
-    lax.fori_loop(0, NDEV, unpack, 0, unroll=4)
+        v = ret_v[within(t // 32, NDEV)]
+        ocean_v[b] = jnp.where(t >= 0, v, 0.0)
+        return carry
+
+    parts = []
+    for n in range(4):
+        lax.fori_loop(32 * n, 32 * n + 32, unpack, 0, unroll=8)
+        part = pl.ds(32 * n, 32)
+        parts.append(pltpu.make_async_copy(ocean_v.at[part], ocean_out.at[part], sem.at[4 + n]))
+        parts[-1].start()
     store.wait()
-    some.wait_send()
+    for part in parts:
+        part.wait()
 
 
 def local(ice_state, thickness, concentration, cat_mask, forcing, ice_target):
     blocks = forcing.reshape(NDEV, 4, 8, 128).transpose(0, 2, 1, 3).reshape(NDEV, 32, 128)
-    hbm = pl.BlockSpec(memory_space=pltpu.HBM)
+    hbm = pl.BlockSpec(memory_space=pl.ANY)
     vmem, dma = pltpu.VMEM, pltpu.SemaphoreType.DMA
 
     def v(*shape, dtype=F32):
@@ -574,16 +598,15 @@
 
     raw = (5, NLON, 1024)
     rows = W * 8
-    ice, ocean = pl.pallas_call(
+    listed = ice_target.reshape(1, NDEV)
+    outs = (jax.ShapeDtypeStruct(raw, F32), jax.ShapeDtypeStruct((NDEV, 16, 128), F32))
+    ice, back = pl.pallas_call(
         kernel,
-        out_shape=(
-            jax.ShapeDtypeStruct(raw, F32),
-            jax.ShapeDtypeStruct((NDEV, 16, 128), F32),
-        ),
+        out_shape=outs,
         in_specs=[hbm] * 6,
-        out_specs=(pl.BlockSpec(memory_space=pl.ANY), pl.BlockSpec(memory_space=vmem)),
+        out_specs=(hbm, hbm),
         scratch_shapes=[
-            pltpu.SMEM((1, 128), jnp.int32), v(1, 128, dtype=jnp.int32),
+            v(1, 128, dtype=jnp.int32),
             v(8, 128, dtype=jnp.int32), pltpu.SMEM((8, 128), jnp.int32),
             v(8, 128, dtype=jnp.int32), pltpu.SMEM((8, 128), jnp.int32),
             v(*raw), v(*raw), v(*raw), v(*raw, dtype=jnp.int32),
@@ -591,15 +614,26 @@
             v(6, rows, 128), v(3, rows, 128), v(4, rows, 128),
             v(5, W, 128), v(3, W, 128), v(4, W, 128),
             v(16, 128), v(3, 16, 128), v(8, 128), v(3, 8, 128), v(16, 128), v(3, 16, 128), v(7, W, 128),
-            v(2, 5, OWN, 128), v(2, 5, OWN, 128),
-            v(2, NLON * 8, 128), v(32, 16, 128), v(NDEV, 16, 128), v(NDEV, 16, 128), v(*raw),
+            v(2, 5, OWN, 128), v(2, 5, OWN, 128), v(2, 7, OWN, 128), v(2, 7, OWN, 128),
+            v(2, NLON * 8, 128), v(32, 16, 128), v(NDEV, 16, 128), v(*raw),
             dma((7,)), dma((4,)), dma((2,)), dma((2,)), dma((17,)), dma((17,)),
         ],
         compiler_params=pltpu.CompilerParams(
             collective_id=0, has_side_effects=True, vmem_limit_bytes=58 * 2**20
         ),
         name="ice",
-    )(ice_target.reshape(1, NDEV), ice_state[0], thickness[0], concentration[0], cat_mask[0], blocks)
+    )(listed, ice_state[0], thickness[0], concentration[0], cat_mask[0], blocks)
+    ice, ocean = pl.pallas_call(
+        hand_out,
+        out_shape=outs,
+        in_specs=[hbm] * 3,
+        out_specs=(hbm, hbm),
+        scratch_shapes=[
+            pltpu.SMEM((1, 128), jnp.int32), v(NDEV, 16, 128), v(*raw), v(NDEV, 16, 128), dma((8,)),
+        ],
+        compiler_params=pltpu.CompilerParams(vmem_limit_bytes=58 * 2**20),
+        name="hand_out",
+    )(listed, ice, back)
     ocean = ocean.reshape(NDEV, 8, 2, 128).transpose(0, 2, 1, 3).reshape(NDEV, 2, 1024)
     return ice[None], ocean
 

time: 89.6 us -> 81.6 us (0.911)
  local copies, waits for them, and re-layouts: 4.25 us -> 0 us
  Pallas kernels: 84.5 us -> 80.9 us
    unnamed x2 -> x0, local copies, waits for them, and re-layouts: 4.25 us -> none
    pallas_call x1 -> x2, Pallas kernels: 84.5 us -> 80.9 us  [the longest x1 77.7 us: local(): pl.pallas_call(kernel, out_shape=outs, in_specs=[hbm] * 6, out_specs=(hbm...]
where the time goes in v3:
time: 81.6 us; the launch traced here: 81.5 us
  Pallas kernels  80.9 us (99%)
    pallas_call x1, Pallas kernels, local(): pl.pallas_call(kernel, out_shape=outs, in_specs=[hbm] * 6, out_specs=(hbm...  77.7 us
    pallas_call x1, Pallas kernels, local(): pl.pallas_call(hand_out, out_shape=outs, in_specs=[hbm] * 3, out_specs=(h...  3.17 us

profile of v3, /device:TPU:1, one launch (start us, length us, event | category | flops | bytes accessed | tf_op | source)
XLA Modules:
  0.0 81.5 jit_solution(7233817680325274953)
XLA Ops:
  0.6 77.7 %ice.1 = (f32[5,32,1024]{2,1,0:T(8,128)}, f32[128,16,128]{2,1,0:T(8,128)}) custom-call(s32[1,128]{1,0:T(1,128)} %bitcast.21, f32[5,32,1024]{2,1,0:T(8,128)} %bitcast.17, f32[5,32,1024]{2,1,0:T(8,128)} %bitcast.18, f32[5,32,1024]{2,1,0:T(8,128)} %bitcast.19, s32[5,32,1024]{2,1,0:T(8,128)} %bitcast.20, f32[128,32,128]{2,1,0:T(8,128)} %bitcast.16), custom_call_target="tpu_custom_call" | custom-call | tf_op jit(solution)/shard_map/ice/pallas_call | solution.py:603
  78.3 3.2 %hand_out.1 = (f32[5,32,1024]{2,1,0:T(8,128)}, f32[128,16,128]{2,1,0:T(8,128)}) custom-call(s32[1,128]{1,0:T(1,128)} %bitcast.22, f32[5,32,1024]{2,1,0:T(8,128)} %get-tuple-element.6.ice, f32[128,16,128]{2,1,0:T(8,128)} %get-tuple-element.7.ret), custom_call_target="tpu_custom_call" | custom-call | tf_op jit(solution)/shard_map/hand_out/pallas_call | solution.py:626

commit v4 on v3

--- a/solution.py
+++ b/solution.py
@@ -17,6 +17,7 @@
 RB = 33
 PER = W // 8
 F32 = jnp.float32
+BODY = 16
 
 
 def at(d):
@@ -287,9 +288,9 @@
             else:
                 pl.when(d != me)(copy.wait_send)
 
-    first = beside(edge7.at[0], edge7.at[1], h7.at[0], h7.at[1], 0) + across(t7, p7, 4)
-    second = halo(fo, 4, 7) + across(t4, p4, 9)
-    third = beside(edge.at[0], edge.at[1], h5.at[0], h5.at[1], 12) + across(t5, p5, 14)
+    first = across(t7, p7, 4) + beside(edge7.at[0], edge7.at[1], h7.at[0], h7.at[1], 0)
+    second = across(t4, p4, 9) + halo(fo, 4, 7)
+    third = across(t5, p5, 14) + beside(edge.at[0], edge.at[1], h5.at[0], h5.at[1], 12)
 
     to_smem.wait()
     loads[5].wait()
@@ -347,64 +348,76 @@
 
     def sweep(lo, hi, body):
         def step(i, carry):
-            body((lo + 4 * i) * 8, 4)
+            body((lo + BODY * i) * 8, BODY)
             return carry
 
-        count = (hi - lo) // 4
-        if count:
+        count = (hi - lo) // BODY
+        if count > 1:
             lax.fori_loop(0, count, step, 0)
-        if (hi - lo) % 4:
-            body((lo + 4 * count) * 8, (hi - lo) % 4)
-
-    def strength_of(volume, cover):
-        return volume * jnp.exp(-2.0 * (1.0 - cover))
-
-    def stress_at(r, n):
-        new = stress(
+        elif count:
+            body(lo * 8, BODY)
+        if (hi - lo) % BODY:
+            body((lo + BODY * count) * 8, (hi - lo) % BODY)
+
+    def stress_of(r, n):
+        return (
             diff_lon(st, 0, r, n), diff_lat(st, 1, r, n), diff_lat(st, 0, r, n), diff_lon(st, 1, r, n),
             get(st, 2, r, n), get(st, 3, r, n), get(st, 4, r, n), get(sc, 2, r, n),
         )
+
+    def stress_to(r, n, new):
         for ch in range(3):
             put(st, 2 + ch, r, n, new[ch])
         put(st, 5, r, n, new[0] - new[1])
 
-    def stress_strip():
-        ue, un = whole(sp, 0), whole(sp, 1)
-        new = stress(
-            strip_lon(ue), strip_lat(un), strip_lat(ue), strip_lon(un),
-            whole(sp, 2), whole(sp, 3), whole(sp, 4), whole(spc, 2),
-        )
-        for ch in range(3):
-            keep(sp, 2 + ch, new[ch])
-
-    def momentum_at(r, n):
+    def stress_at(r, n):
+        stress_to(r, n, stress(*stress_of(r, n)))
+
+    def momentum_of(r, n):
         dxx = diff_lon(st, 2, r, n) + diff_lon(st, 3, r, n)
-        new = momentum(
+        return (
             get(st, 0, r, n), get(st, 1, r, n),
             dxx, diff_lat(st, 4, r, n), diff_lon(st, 4, r, n), diff_lat(st, 5, r, n),
             get(fo, 0, r, n), get(fo, 1, r, n), get(fo, 2, r, n), get(fo, 3, r, n), get(sc, 0, r, n), get(sc, 1, r, n),
         )
+
+    def momentum_to(r, n, new):
         put(st, 0, r, n, new[0])
         put(st, 1, r, n, new[1])
 
-    def momentum_strip():
+    def momentum_at(r, n):
+        momentum_to(r, n, momentum(*momentum_of(r, n)))
+
+    def stress_of_strip():
+        ue, un = whole(sp, 0), whole(sp, 1)
+        return (
+            strip_lon(ue), strip_lat(un), strip_lat(ue), strip_lon(un),
+            whole(sp, 2), whole(sp, 3), whole(sp, 4), whole(spc, 2),
+        )
+
+    def momentum_of_strip():
         ss, sd, sh = whole(sp, 2), whole(sp, 3), whole(sp, 4)
-        new = momentum(
+        return (
             whole(sp, 0), whole(sp, 1), strip_lon(ss + sd), strip_lat(sh), strip_lon(sh), strip_lat(ss - sd),
             whole(spf, 0), whole(spf, 1), whole(spf, 2), whole(spf, 3), whole(spc, 0), whole(spc, 1),
         )
-        keep(sp, 0, new[0])
-        keep(sp, 1, new[1])
+
+    def rims(lon, of, of_strip, step, to, channel):
+        near, far = lon * 8, (W - lon - H) * 8
+        parts = zip(of(near, H), of(far, H), of_strip(), strict=True)
+        new = step(*[jnp.concatenate([a, b, c.reshape(PER * 8, 128)], axis=0) for a, b, c in parts])
+        to(near, H, [v[0:OWN] for v in new])
+        to(far, H, [v[OWN : 2 * OWN] for v in new])
+        for n, v in enumerate(new):
+            sp[channel + n] = v[2 * OWN :]
+
+    def strength_of(volume, cover):
+        return volume * jnp.exp(-2.0 * (1.0 - cover))
 
     def statics(r, n):
         cover, volume = get(sc, 0, r, n), get(sc, 1, r, n)
         put(sc, 1, r, n, volume + 0.5)
         put(sc, 2, r, n, strength_of(volume, cover))
-
-    def rims(first_lon, width, body):
-        for lon in (first_lon, W - first_lon - width):
-            for n in range(0, width, 4):
-                body((lon + n) * 8, min(4, width - n))
 
     def inner(done):
         for m in range(HALF):
@@ -413,10 +426,8 @@
             sweep(H + 2 + 2 * m, W - H - 2 - 2 * m, momentum_at)
 
     def outer(m, carry):
-        rims(1 + 2 * m, H, stress_at)
-        stress_strip()
-        rims(2 + 2 * m, H, momentum_at)
-        momentum_strip()
+        rims(1 + 2 * m, stress_of, stress_of_strip, stress, stress_to, 2)
+        rims(2 + 2 * m, momentum_of, momentum_of_strip, momentum, momentum_to, 0)
         return carry
 
     strip_own(sp, st, 5)
@@ -471,7 +482,8 @@
     strip_far(sp, 0, 5)
     strip_own(spc, sc, 2, True)
     strip_far(spc, 5, 2)
-    rims(0, H, statics)
+    statics(0, H)
+    statics(END, H)
     cover, volume = whole(spc, 0), whole(spc, 1)
     keep(spc, 1, volume + 0.5)
     keep(spc, 2, strength_of(volume, cover))

time: 81.6 us -> 75.9 us (0.930)
  Pallas kernels: 80.9 us -> 75.1 us
    pallas_call x1, Pallas kernels: 77.7 us -> 71.9 us  [local(): pl.pallas_call(kernel, out_shape=outs, in_specs=[hbm] * 6, out_specs=(hbm...]
where the time goes in v4:
time: 75.9 us; the launch traced here: 75.7 us
  Pallas kernels  75.1 us (99%)
    pallas_call x1, Pallas kernels, local(): pl.pallas_call(kernel, out_shape=outs, in_specs=[hbm] * 6, out_specs=(hbm...  71.9 us
    pallas_call x1, Pallas kernels, local(): pl.pallas_call(hand_out, out_shape=outs, in_specs=[hbm] * 3, out_specs=(h...  3.17 us

profile of v4, /device:TPU:1, one launch (start us, length us, event | category | flops | bytes accessed | tf_op | source)
XLA Modules:
  0.0 75.7 jit_solution(7900670322136234402)
XLA Ops:
  0.6 71.9 %ice.1 = (f32[5,32,1024]{2,1,0:T(8,128)}, f32[128,16,128]{2,1,0:T(8,128)}) custom-call(s32[1,128]{1,0:T(1,128)} %bitcast.21, f32[5,32,1024]{2,1,0:T(8,128)} %bitcast.17, f32[5,32,1024]{2,1,0:T(8,128)} %bitcast.18, f32[5,32,1024]{2,1,0:T(8,128)} %bitcast.19, s32[5,32,1024]{2,1,0:T(8,128)} %bitcast.20, f32[128,32,128]{2,1,0:T(8,128)} %bitcast.16), custom_call_target="tpu_custom_call" | custom-call | tf_op jit(solution)/shard_map/ice/pallas_call | solution.py:615
  72.5 3.2 %hand_out.1 = (f32[5,32,1024]{2,1,0:T(8,128)}, f32[128,16,128]{2,1,0:T(8,128)}) custom-call(s32[1,128]{1,0:T(1,128)} %bitcast.22, f32[5,32,1024]{2,1,0:T(8,128)} %get-tuple-element.6.ice, f32[128,16,128]{2,1,0:T(8,128)} %get-tuple-element.7.ret), custom_call_target="tpu_custom_call" | custom-call | tf_op jit(solution)/shard_map/hand_out/pallas_call | solution.py:638

commit v5 on v4

--- a/solution.py
+++ b/solution.py
@@ -20,6 +20,15 @@
 BODY = 16
 
 
+def spread():
+    hops = (0, 1, 2, 1)
+    ways = [(n * 37) % NDEV for n in range(1, NDEV)]
+    return sorted(ways, key=lambda k: -(hops[k % 4] + hops[k // 8 % 4] + hops[k // 32]))
+
+
+ORDER = spread()
+
+
 def at(d):
     return (d // 4, d % 4)
 
@@ -96,30 +105,14 @@
     def flipped(bit, by):
         return 1 - bit if by else bit
 
-    low = []
-    for n in range(16):
-        n = (n * 11) % 16
-        px = 2 * flipped(x // 2, (n // 2) % 2) + flipped(x % 2, n % 2)
-        low.append((2 * flipped(z % 2, (n // 8) % 2) + flipped(core, (n // 4) % 2), px))
+    xs = [2 * flipped(x // 2, n // 2) + flipped(x % 2, n % 2) for n in range(4)]
+    zs = [4 * flipped(z // 2, n // 2) + 2 * flipped(z % 2, n % 2) for n in range(4)]
+    ys = [16 * flipped(y // 2, n // 2) + 8 * flipped(y % 2, n % 2) for n in range(4)]
+    cs = [core, 1 - core]
 
     def for_peers(act):
-        def turn(q, carry):
-            high = []
-            for r in range(8):
-                m = (q + r) % 8
-                z1 = (z // 2 + m) % 2
-                y0 = (y + m // 2) % 2
-                y1 = (y // 2 + m // 4) % 2
-                high.append(8 * (2 * y1 + y0) + 4 * z1)
-            for n in range(16):
-                a, b = high[(3 * n) % 8] + low[n][0], low[n][1]
-                if n:
-                    act(a, b)
-                else:
-                    pl.when(q != 0)(lambda a=a, b=b: act(a, b))
-            return carry
-
-        lax.fori_loop(0, 8, turn, 0)
+        for k in ORDER:
+            act(ys[k // 32] + zs[k // 8 % 4] + cs[k // 4 % 2], xs[k % 4])
 
     loads = [
         pltpu.make_async_copy(src, dst, in_sem.at[i])
@@ -256,11 +249,11 @@
             (remote(to_east, at_west, east, i + 1), None, None),
         ]
 
-    def halo(ref, count, i):
+    def halo(ref, count, width, i):
         def part(lon):
-            return ref.at[pl.ds(0, count), pl.ds(lon * 8, OWN)]
-
-        return beside(part(H), part(NLON), part(0), part(H + NLON), i)
+            return ref.at[pl.ds(0, count), pl.ds(lon * 8, width * 8)]
+
+        return beside(part(H), part(H + NLON - width), part(H - width), part(H + NLON), i)
 
     def across(t, p, i):
         parts = []
@@ -289,7 +282,7 @@
                 pl.when(d != me)(copy.wait_send)
 
     first = across(t7, p7, 4) + beside(edge7.at[0], edge7.at[1], h7.at[0], h7.at[1], 0)
-    second = across(t4, p4, 9) + halo(fo, 4, 7)
+    second = across(t4, p4, 9) + halo(fo, 4, H - 2, 7)
     third = across(t5, p5, 14) + beside(edge.at[0], edge.at[1], h5.at[0], h5.at[1], 12)
 
     to_smem.wait()
@@ -466,9 +459,11 @@
                 fo[ch, pl.ds(OWN + p * 8 + chunk, 8, stride=32), :] = rows[p]
         return carry
 
-    lax.fori_loop(0, 8, place_rows, 0, unroll=2)
+    place_rows(7, 0)
     tops(t4, [(fo, 0, -1), (fo, 1, -1), (fo, 2, -1), (fo, 3, -1)])
-    start(second)
+    start(second[:3])
+    lax.fori_loop(0, 7, place_rows, 0, unroll=7)
+    start(second[3:])
 
     inner(1)
 
@@ -495,10 +490,11 @@
     lax.fori_loop(0, HALF, outer, 0)
     merge()
     tops(t5, state_parts)
+    start(third[:3])
     for ch in range(5):
         edge[0, ch] = st[ch, OWN : 2 * OWN, :]
         edge[1, ch] = st[ch, END - OWN : END, :]
-    start(third)
+    start(third[3:])
     strip_own(sp, st, 5)
     inner(0)
 
@@ -529,7 +525,7 @@
                 sb[chunk * 4 + j, pl.ds(ch, 8, stride=2), :] = rows[j]
         return carry
 
-    lax.fori_loop(0, 8, blocks, 0, unroll=4)
+    lax.fori_loop(0, 8, blocks, 0, unroll=8)
 
     def give(a, b):
         d = a * 4 + b

time: 75.9 us -> 74.2 us (0.978)
  Pallas kernels: 75.1 us -> 73.4 us
    pallas_call x1, Pallas kernels: 71.9 us -> 70.3 us  [local(): pl.pallas_call(kernel, out_shape=outs, in_specs=[hbm] * 6, out_specs=(hbm...]
where the time goes in v5:
time: 74.2 us; the launch traced here: 74.1 us
  Pallas kernels  73.4 us (99%)
    pallas_call x1, Pallas kernels, local(): pl.pallas_call(kernel, out_shape=outs, in_specs=[hbm] * 6, out_specs=(hbm...  70.3 us
    pallas_call x1, Pallas kernels, local(): pl.pallas_call(hand_out, out_shape=outs, in_specs=[hbm] * 3, out_specs=(h...  3.17 us

profile of v5, /device:TPU:1, one launch (start us, length us, event | category | flops | bytes accessed | tf_op | source)
XLA Modules:
  0.0 74.1 jit_solution(15089337656246842117)
XLA Ops:
  0.6 70.3 %ice.1 = (f32[5,32,1024]{2,1,0:T(8,128)}, f32[128,16,128]{2,1,0:T(8,128)}) custom-call(s32[1,128]{1,0:T(1,128)} %bitcast.21, f32[5,32,1024]{2,1,0:T(8,128)} %bitcast.17, f32[5,32,1024]{2,1,0:T(8,128)} %bitcast.18, f32[5,32,1024]{2,1,0:T(8,128)} %bitcast.19, s32[5,32,1024]{2,1,0:T(8,128)} %bitcast.20, f32[128,32,128]{2,1,0:T(8,128)} %bitcast.16), custom_call_target="tpu_custom_call" | custom-call | tf_op jit(solution)/shard_map/ice/pallas_call | solution.py:611
  70.9 3.2 %hand_out.1 = (f32[5,32,1024]{2,1,0:T(8,128)}, f32[128,16,128]{2,1,0:T(8,128)}) custom-call(s32[1,128]{1,0:T(1,128)} %bitcast.22, f32[5,32,1024]{2,1,0:T(8,128)} %get-tuple-element.6.ice, f32[128,16,128]{2,1,0:T(8,128)} %get-tuple-element.7.ret), custom_call_target="tpu_custom_call" | custom-call | tf_op jit(solution)/shard_map/hand_out/pallas_call | solution.py:634

commit v6 on v5

--- a/solution.py
+++ b/solution.py
@@ -22,8 +22,12 @@
 
 def spread():
     hops = (0, 1, 2, 1)
-    ways = [(n * 37) % NDEV for n in range(1, NDEV)]
-    return sorted(ways, key=lambda k: -(hops[k % 4] + hops[k // 8 % 4] + hops[k // 32]))
+    ways = [(n * 53) % NDEV for n in range(1, NDEV)]
+
+    def far(k):
+        return 2 * (hops[k % 4] + hops[k // 8 % 4] + hops[k // 32]) + k // 4 % 2
+
+    return sorted(ways, key=far, reverse=True)
 
 
 ORDER = spread()
@@ -128,16 +132,7 @@
     def greet(a, b):
         pl.semaphore_signal(barrier, inc=1, device_id=(a, b), device_id_type=MESH)
 
-    for b in range(1, 4):
-        greet(gx, (gy + b) % 4)
-
-    def greet_all(k, carry):
-        a = (gx + k) % 32
-        for b in range(4):
-            greet(a, b)
-        return carry
-
-    lax.fori_loop(1, 32, greet_all, 0)
+    for_peers(greet)
 
     square = (NDEV, NDEV)
     lane_sq, sub_sq = iota(square, 1), iota(square, 0)
@@ -482,8 +477,9 @@
     cover, volume = whole(spc, 0), whole(spc, 1)
     keep(spc, 1, volume + 0.5)
     keep(spc, 2, strength_of(volume, cover))
-    landed(second)
+    landed(second[:3])
     beyond(p4, 4)
+    landed(second[3:])
     strip_own(spf, fo, 4)
     strip_far(spf, 0, 4)
 
@@ -498,11 +494,12 @@
     strip_own(sp, st, 5)
     inner(0)
 
-    landed(third)
+    landed(third[:3])
+    beyond(p5, 5)
+    landed(third[3:])
     for ch in range(5):
         st[ch, 0:OWN, :] = h5[0, ch]
         st[ch, END:, :] = h5[1, ch]
-    beyond(p5, 5)
     strip_own(sp, st, 5, True)
     strip_far(sp, 0, 5)
 

time: 74.2 us -> 72.8 us (0.981)
  Pallas kernels: 73.4 us -> 72 us
    pallas_call x1, Pallas kernels: 70.3 us -> 68.8 us  [local(): pl.pallas_call(kernel, out_shape=outs, in_specs=[hbm] * 6, out_specs=(hbm...]
where the time goes in v6:
time: 72.8 us; the launch traced here: 72.6 us
  Pallas kernels  72 us (99%)
    pallas_call x1, Pallas kernels, local(): pl.pallas_call(kernel, out_shape=outs, in_specs=[hbm] * 6, out_specs=(hbm...  68.8 us
    pallas_call x1, Pallas kernels, local(): pl.pallas_call(hand_out, out_shape=outs, in_specs=[hbm] * 3, out_specs=(h...  3.17 us

profile of v6, /device:TPU:1, one launch (start us, length us, event | category | flops | bytes accessed | tf_op | source)
XLA Modules:
  0.0 72.6 jit_solution(3409623182987852461)
XLA Ops:
  0.6 68.8 %ice.1 = (f32[5,32,1024]{2,1,0:T(8,128)}, f32[128,16,128]{2,1,0:T(8,128)}) custom-call(s32[1,128]{1,0:T(1,128)} %bitcast.21, f32[5,32,1024]{2,1,0:T(8,128)} %bitcast.17, f32[5,32,1024]{2,1,0:T(8,128)} %bitcast.18, f32[5,32,1024]{2,1,0:T(8,128)} %bitcast.19, s32[5,32,1024]{2,1,0:T(8,128)} %bitcast.20, f32[128,32,128]{2,1,0:T(8,128)} %bitcast.16), custom_call_target="tpu_custom_call" | custom-call | tf_op jit(solution)/shard_map/ice/pallas_call | solution.py:608
  69.5 3.2 %hand_out.1 = (f32[5,32,1024]{2,1,0:T(8,128)}, f32[128,16,128]{2,1,0:T(8,128)}) custom-call(s32[1,128]{1,0:T(1,128)} %bitcast.22, f32[5,32,1024]{2,1,0:T(8,128)} %get-tuple-element.6.ice, f32[128,16,128]{2,1,0:T(8,128)} %get-tuple-element.7.ret), custom_call_target="tpu_custom_call" | custom-call | tf_op jit(solution)/shard_map/hand_out/pallas_call | solution.py:631

commit v7 on v6

--- a/solution.py
+++ b/solution.py
@@ -95,7 +95,7 @@
 
 def kernel(
     tgt, state, thick, conc, mask, forc, ice_out, ret,
-    tgt_v, idx_v, idx_s, dst_v, dst_s,
+    tgt_v, idx_v, idx_s, dst_v, dst_s, back_v, back_s,
     r_state, r_thick, r_conc, r_mask, fv, outb, arr, tagm,
     st, sc, fo, sp, spc, spf,
     t7, p7, t4, p4, t5, p5, ext, edge, h5, edge7, h7,
@@ -434,15 +434,17 @@
         tagm[pl.ds(s, 1), :] = arr[s, 32:33, :]
         return carry
 
-    lax.fori_loop(0, NDEV, tag, 0, unroll=8)
+    lax.fori_loop(0, NDEV, tag, 0, unroll=32)
     tags = tagm[...]
     origin = jnp.sum(jnp.where(tags.astype(jnp.int32) == lane_sq, sub_sq.astype(F32), 0.0), axis=0, keepdims=True)
     back = jnp.sum(jnp.where(sub_sq == lane_sq, tags, 0.0), axis=0, keepdims=True)
     dst_v[0:1, :] = origin.astype(jnp.int32)
-    dst_v[1:2, :] = jnp.maximum(back, 0.0).astype(jnp.int32)
     to_smem = pltpu.make_async_copy(dst_v, dst_s, loc_sem.at[2])
     to_smem.start()
+    back_v[0:1, :] = jnp.maximum(back, 0.0).astype(jnp.int32)
     to_smem.wait()
+    to_smem = pltpu.make_async_copy(back_v, back_s, loc_sem.at[2])
+    to_smem.start()
 
     group8 = lane8 // 32
 
@@ -483,7 +485,7 @@
     strip_own(spf, fo, 4)
     strip_far(spf, 0, 4)
 
-    lax.fori_loop(0, HALF, outer, 0)
+    lax.fori_loop(0, HALF, outer, 0, unroll=2)
     merge()
     tops(t5, state_parts)
     start(third[:3])
@@ -503,7 +505,7 @@
     strip_own(sp, st, 5, True)
     strip_far(sp, 0, 5)
 
-    lax.fori_loop(0, HALF, outer, 0)
+    lax.fori_loop(0, HALF, outer, 0, unroll=2)
     merge()
 
     def drag(r, n):
@@ -524,16 +526,18 @@
 
     lax.fori_loop(0, 8, blocks, 0, unroll=8)
 
+    to_smem.wait()
+
     def give(a, b):
         d = a * 4 + b
-        out2[d] = sb[within(dst_s[1, d], 32)]
+        out2[d] = sb[within(back_s[0, d], 32)]
         pltpu.make_async_remote_copy(
             src_ref=out2.at[d], dst_ref=ret.at[me], send_sem=r_sem.at[0], recv_sem=r_sem.at[1],
             device_id=(a, b), device_id_type=MESH,
         ).start()
 
     for_peers(give)
-    out2[me] = sb[within(dst_s[1, me], 32)]
+    out2[me] = sb[within(back_s[0, me], 32)]
     own_stress = pltpu.make_async_copy(out2.at[me], ret.at[me], loc_sem.at[1])
     own_stress.start()
 
@@ -612,6 +616,7 @@
         out_specs=(hbm, hbm),
         scratch_shapes=[
             v(1, 128, dtype=jnp.int32),
+            v(8, 128, dtype=jnp.int32), pltpu.SMEM((8, 128), jnp.int32),
             v(8, 128, dtype=jnp.int32), pltpu.SMEM((8, 128), jnp.int32),
             v(8, 128, dtype=jnp.int32), pltpu.SMEM((8, 128), jnp.int32),
             v(*raw), v(*raw), v(*raw), v(*raw, dtype=jnp.int32),

time: 72.8 us -> 72.7 us (level)
  no operation moved by 1% of the time
where the time goes in v7:
time: 72.7 us; the launch traced here: 72.5 us
  Pallas kernels  71.9 us (99%)
    pallas_call x1, Pallas kernels, local(): pl.pallas_call(kernel, out_shape=outs, in_specs=[hbm] * 6, out_specs=(hbm...  68.7 us
    pallas_call x1, Pallas kernels, local(): pl.pallas_call(hand_out, out_shape=outs, in_specs=[hbm] * 3, out_specs=(h...  3.17 us

profile of v7, /device:TPU:1, one launch (start us, length us, event | category | flops | bytes accessed | tf_op | source)
XLA Modules:
  0.0 72.5 jit_solution(16858678917662385325)
XLA Ops:
  0.6 68.7 %ice.1 = (f32[5,32,1024]{2,1,0:T(8,128)}, f32[128,16,128]{2,1,0:T(8,128)}) custom-call(s32[1,128]{1,0:T(1,128)} %bitcast.21, f32[5,32,1024]{2,1,0:T(8,128)} %bitcast.17, f32[5,32,1024]{2,1,0:T(8,128)} %bitcast.18, f32[5,32,1024]{2,1,0:T(8,128)} %bitcast.19, s32[5,32,1024]{2,1,0:T(8,128)} %bitcast.20, f32[128,32,128]{2,1,0:T(8,128)} %bitcast.16), custom_call_target="tpu_custom_call" | custom-call | tf_op jit(solution)/shard_map/ice/pallas_call | solution.py:612
  69.4 3.2 %hand_out.1 = (f32[5,32,1024]{2,1,0:T(8,128)}, f32[128,16,128]{2,1,0:T(8,128)}) custom-call(s32[1,128]{1,0:T(1,128)} %bitcast.22, f32[5,32,1024]{2,1,0:T(8,128)} %get-tuple-element.6.ice, f32[128,16,128]{2,1,0:T(8,128)} %get-tuple-element.7.ret), custom_call_target="tpu_custom_call" | custom-call | tf_op jit(solution)/shard_map/hand_out/pallas_call | solution.py:636

commit v8 on v6

--- a/solution.py
+++ b/solution.py
@@ -25,7 +25,8 @@
     ways = [(n * 53) % NDEV for n in range(1, NDEV)]
 
     def far(k):
-        return 2 * (hops[k % 4] + hops[k // 8 % 4] + hops[k // 32]) + k // 4 % 2
+        along = hops[k % 4], hops[k // 8 % 4], hops[k // 32]
+        return 8 * sum(along) + 4 * (k // 4 % 2) + max(along)
 
     return sorted(ways, key=far, reverse=True)
 

time: 72.8 us -> 72.8 us (level)
  no operation moved by 1% of the time
where the time goes in v8:
time: 72.8 us; the launch traced here: 72.7 us
  Pallas kernels  72 us (99%)
    pallas_call x1, Pallas kernels, local(): pl.pallas_call(kernel, out_shape=outs, in_specs=[hbm] * 6, out_specs=(hbm...  68.9 us
    pallas_call x1, Pallas kernels, local(): pl.pallas_call(hand_out, out_shape=outs, in_specs=[hbm] * 3, out_specs=(h...  3.17 us

profile of v8, /device:TPU:1, one launch (start us, length us, event | category | flops | bytes accessed | tf_op | source)
XLA Modules:
  0.0 72.7 jit_solution(10435018884045663520)
XLA Ops:
  0.6 68.9 %ice.1 = (f32[5,32,1024]{2,1,0:T(8,128)}, f32[128,16,128]{2,1,0:T(8,128)}) custom-call(s32[1,128]{1,0:T(1,128)} %bitcast.21, f32[5,32,1024]{2,1,0:T(8,128)} %bitcast.17, f32[5,32,1024]{2,1,0:T(8,128)} %bitcast.18, f32[5,32,1024]{2,1,0:T(8,128)} %bitcast.19, s32[5,32,1024]{2,1,0:T(8,128)} %bitcast.20, f32[128,32,128]{2,1,0:T(8,128)} %bitcast.16), custom_call_target="tpu_custom_call" | custom-call | tf_op jit(solution)/shard_map/ice/pallas_call | solution.py:609
  69.5 3.2 %hand_out.1 = (f32[5,32,1024]{2,1,0:T(8,128)}, f32[128,16,128]{2,1,0:T(8,128)}) custom-call(s32[1,128]{1,0:T(1,128)} %bitcast.22, f32[5,32,1024]{2,1,0:T(8,128)} %get-tuple-element.6.ice, f32[128,16,128]{2,1,0:T(8,128)} %get-tuple-element.7.ret), custom_call_target="tpu_custom_call" | custom-call | tf_op jit(solution)/shard_map/hand_out/pallas_call | solution.py:632
